TPU v7x, 256 devices: a whole 4x4x8 slice. The times are simulated.
256 devices in a mesh: sec: 2 (over y_lo), ri: 64 (over z, x, core), ao: 2 (over y_hi).
Axes of the slice: x: 4, y: 4 (y_hi: 2, y_lo: 2; y = y_hi * 2 + y_lo), z: 8, core: 2. Of those that a mesh axis runs over, the one named last changes fastest.
Arguments:
- coulomb_band: bfloat16 [16384, 768], P('ri'), may hold values from -0.21875 to 0.21875
- band_mask: int32 [256, 12], P('ri'), may hold values from 0 to 1, as said below
- dielectric: bfloat16 [2, 16384, 1024], P('sec', 'ri', 'ao'), may hold values from -6 to 6
- three_centre: bfloat16 [16384, 128, 128], P('ri', 'sec'), may hold values from -0.099121094 to 0.099121094
- centre_mask: int32 [256], P('ri'), may hold values 0 or 1
- greens: bfloat16 [2, 512, 512], P('sec', 'ao'), may hold values from -0.5 to 0.5
- tile_map: int32 [64, 1], replicated, may hold values from 0 to 3
- batch_order: int32 [2, 64], replicated, may hold values from 0 to 63, each once within a row
Outputs:
- self_energy: float32 [2, 512, 512], P('sec', ('ri', 'ao'))
Inputs may be any that keep to these rules, and one draw needn't show every extreme that they name: `band_mask`: in every row of tiles, the tile on the block's diagonal within the lower neighbour's 256 columns and within the upper neighbour's 256 columns is 1. `batch_order`: each row names every block once. `tile_map`: every AO tile is the tile of some block.
All inputs are finite; a program needn't handle non-finite values. No bound on the sum of `centre_mask` on one device may be relied on, other than what follows from the above.
Results may differ from a plain program's by a relative error of at most 0.0049.
Values may be sent and summed in bfloat16 or wider, within the bound.
No kernel may reach another device: no remote copies, remote signals or barrier semaphores. Data moves between devices by JAX's collectives and lax.ppermute only.
A program may use at most 192 MiB of HBM per device.

v0:
```python
import jax
import jax.numpy as jnp
from jax import lax
from jax.experimental import pallas as pl
from jax.experimental.pallas import tpu as pltpu
from jax.sharding import Mesh, PartitionSpec as P

NZ, NX, NC = 8, 4, 2
CHIPS = NZ * NX
VMEM = 60 << 20
BF = jnp.bfloat16
F32 = jnp.float32


def shift(value, axis, by):
    n = lax.axis_size(axis)
    return lax.ppermute(value, axis, [(i, (i + by) % n) for i in range(n)])


def along_y():
    pairs = []
    for y in range(4):
        for core, to in ((0, (y + 1) % 4), (1, (y + 3) % 4)):
            pairs.append(tuple(((p % 2) * NC + core) * 2 + p // 2 for p in (y, to)))
    return pairs


def y_kernel(wt_ref, g_ref, m_ref, y_ref):
    lane = m_ref.shape[2]
    m = jnp.swapaxes(m_ref[...], 0, 1)
    wt = wt_ref[...]
    g = g_ref[0]
    ys = []
    for mu in range(0, m.shape[0], 2):
        s = jnp.dot(wt, jnp.concatenate([m[mu], m[mu + 1]], axis=1), preferred_element_type=F32).astype(BF)
        y = jnp.dot(s, g, preferred_element_type=F32).astype(BF)
        ys += [y[:, :lane], y[:, lane:]]
    y_ref[...] = jnp.swapaxes(jnp.stack(ys), 0, 1)


def y_part(before, part, wt, g2, block):
    rows, mus, lane = block.shape
    group = 16
    steps = mus // group
    specs = [
        pl.BlockSpec((rows, rows), lambda i: (0, 0)),
        pl.BlockSpec((1, 2 * lane, 2 * lane), lambda i: (part % 2, 0, 0)),
        pl.BlockSpec((rows, group, lane), lambda i: (0, i, 0)),
    ]
    args = [wt, g2, block]
    aliases = {}
    kernel = y_kernel
    if before is not None:
        specs.append(pl.BlockSpec(memory_space=pl.ANY))
        args.append(before)
        aliases = {3: 0}

        def kernel(w, g, m, unused, *rest):
            y_kernel(w, g, m, *rest)

    return pl.pallas_call(
        kernel,
        grid=(steps,),
        in_specs=specs,
        out_specs=pl.BlockSpec((rows, group, lane), lambda i: (0, part * steps + i, 0)),
        out_shape=jax.ShapeDtypeStruct((rows, 4 * mus, lane), BF),
        input_output_aliases=aliases,
        compiler_params=pltpu.CompilerParams(vmem_limit_bytes=VMEM),
        cost_estimate=pl.CostEstimate(flops=40 * rows * rows * mus * lane, bytes_accessed=80 * rows * mus * lane, transcendentals=0),
        name="y_part",
    )(*args)


def after(value, *others, weight=0):
    return pl.pallas_call(
        lambda *refs: None,
        in_specs=[pl.BlockSpec(memory_space=pl.ANY)] * (1 + len(others)),
        out_specs=pl.BlockSpec(memory_space=pl.ANY),
        out_shape=jax.ShapeDtypeStruct(value.shape, value.dtype),
        input_output_aliases={0: 0},
        compiler_params=pltpu.CompilerParams(vmem_limit_bytes=VMEM),
        cost_estimate=pl.CostEstimate(
            flops=weight * 1000000000, bytes_accessed=weight * 3000000, transcendentals=0
        ),
        name="after",
    )(value, *others)


def contract_kernel(counts, more, tab_ref, *refs):
    out_ref = refs[-1]
    pieces = sum(counts)
    q = refs[0].shape[0]

    @pl.when(pl.program_id(0) == 0)
    def _():
        out_ref[...] = refs[-2][...] if more else jnp.zeros_like(out_ref)

    acc = out_ref[...]
    place = 0
    for source, count in enumerate(counts):
        f_ref = refs[pieces + source]
        for piece in range(count):
            y_ref = refs[place]
            place += 1
            for i in range(0, q, 2):
                lhs = jnp.concatenate([y_ref[i], y_ref[i + 1]], axis=1)
                rhs = jnp.concatenate([f_ref[piece * q + i], f_ref[piece * q + i + 1]], axis=1)
                acc += lax.dot_general(lhs, rhs, (((1,), (1,)), ((), ())), preferred_element_type=F32)
    out_ref[...] = acc


def contract(before, ys, table, chunks, q, steps=2):
    values = [value for value, _ in chunks]
    counts = [value.shape[0] // q // steps for value in values]
    per = sum(counts)
    rows, lane = ys.shape[1], ys.shape[2]
    nus = values[0].shape[1]

    def y_spec(start, count):
        return pl.BlockSpec((q, rows, lane), lambda i, tab: (tab[start + i * count], 0, 0))

    specs = [
        y_spec(start + piece, count)
        for (_, start), count in zip(chunks, counts)
        for piece in range(count)
    ]
    specs += [pl.BlockSpec((count * q, nus, lane), lambda i, tab: (i, 0, 0)) for count in counts]
    args = [table] + [ys] * per + values
    if before is not None:
        specs.append(pl.BlockSpec((rows, nus), lambda i, tab: (0, 0)))
        args.append(before)
    return pl.pallas_call(
        lambda *refs: contract_kernel(counts, before is not None, *refs),
        grid_spec=pltpu.PrefetchScalarGridSpec(
            num_scalar_prefetch=1,
            grid=(steps,),
            in_specs=specs,
            out_specs=pl.BlockSpec((rows, nus), lambda i, tab: (0, 0)),
        ),
        out_shape=jax.ShapeDtypeStruct((rows, nus), F32),
        compiler_params=pltpu.CompilerParams(vmem_limit_bytes=VMEM),
        cost_estimate=pl.CostEstimate(
            flops=2 * rows * nus * lane * q * per * steps,
            bytes_accessed=2 * q * per * steps * lane * (rows + nus),
            transcendentals=0,
        ),
        name="contract",
    )(*args)


def pick(buffer, table, count, others):
    block = (1,) + buffer.shape[1:]
    zeros = (0,) * (buffer.ndim - 1)

    def spec(i):
        return pl.BlockSpec(block, lambda j, tab: (tab[i],) + zeros)

    def kernel(tab_ref, *refs):
        for i in range(count):
            refs[-1][i] = refs[i][0]

    return pl.pallas_call(
        kernel,
        grid_spec=pltpu.PrefetchScalarGridSpec(
            num_scalar_prefetch=1,
            grid=(1,),
            in_specs=[spec(i) for i in range(count)] + [pl.BlockSpec(memory_space=pl.ANY)] * len(others),
            out_specs=pl.BlockSpec((count,) + buffer.shape[1:], lambda j, tab: (0,) + zeros),
        ),
        out_shape=jax.ShapeDtypeStruct((count,) + buffer.shape[1:], buffer.dtype),
        compiler_params=pltpu.CompilerParams(vmem_limit_bytes=VMEM),
        cost_estimate=pl.CostEstimate(flops=1000, bytes_accessed=1000, transcendentals=0),
        name="pick",
    )(table, *([buffer] * count), *others)


def masked_rows(value, half, mask):
    groups = mask.shape[0]
    steps = 2
    rows = value.shape[0] // 2
    step_rows = rows // steps
    table = jnp.concatenate([half.reshape(1), mask]).astype(jnp.int32)
    block = (step_rows,) + value.shape[1:]

    def kernel(tab_ref, in_ref, out_ref):
        row = tab_ref[0] * rows + pl.program_id(0) * step_rows
        keep = tab_ref[1 + row // (value.shape[0] // groups)].astype(F32)
        out_ref[...] = (in_ref[...].astype(F32) * keep).astype(BF)

    return pl.pallas_call(
        kernel,
        grid_spec=pltpu.PrefetchScalarGridSpec(
            num_scalar_prefetch=1,
            grid=(steps,),
            in_specs=[pl.BlockSpec(block, lambda i, tab: (tab[0] * steps + i, 0, 0))],
            out_specs=pl.BlockSpec(block, lambda i, tab: (i, 0, 0)),
        ),
        out_shape=jax.ShapeDtypeStruct((rows,) + value.shape[1:], BF),
        compiler_params=pltpu.CompilerParams(vmem_limit_bytes=VMEM),
        cost_estimate=pl.CostEstimate(flops=1000, bytes_accessed=1000, transcendentals=0),
        name="masked_rows",
    )(table, value)


def g_kernel(tab_ref, own_ref, oth_ref, out_ref):
    tile = tab_ref[pl.program_id(0)]
    mine = tile // 2 == tab_ref[3]
    g = jnp.where(mine, own_ref[...].astype(F32), oth_ref[...].astype(F32)).astype(BF)
    n = g.shape[0]
    out_ref[...] = jnp.zeros_like(out_ref)
    out_ref[0, :n, :n] = g
    out_ref[0, n:, n:] = g


def g_pairs(own, other, table, width):
    def spec():
        return pl.BlockSpec((width, width), lambda i, tab: (tab[i] % 2, tab[2]))

    return pl.pallas_call(
        g_kernel,
        grid_spec=pltpu.PrefetchScalarGridSpec(
            num_scalar_prefetch=1,
            grid=(2,),
            in_specs=[spec(), spec()],
            out_specs=pl.BlockSpec((1, 2 * width, 2 * width), lambda i, tab: (i, 0, 0)),
        ),
        out_shape=jax.ShapeDtypeStruct((2, 2 * width, 2 * width), BF),
        compiler_params=pltpu.CompilerParams(vmem_limit_bytes=VMEM),
        cost_estimate=pl.CostEstimate(flops=1000, bytes_accessed=1000, transcendentals=0),
        name="g_pairs",
    )(table, own, other)


def body(
    coulomb_band, band_mask, dielectric, three_centre, centre_mask, greens, tile_map, batch_order
):
    rows = coulomb_band.shape[0]
    mus = three_centre.shape[1]
    width = three_centre.shape[2]
    z, x, c = lax.axis_index("z"), lax.axis_index("x"), lax.axis_index("core")
    s, h = lax.axis_index("sec"), lax.axis_index("ao")
    ri = (z * NX + x) * NC + c
    tiles = tile_map[:, 0]
    keep = jnp.repeat(centre_mask, rows // centre_mask.shape[0]).astype(BF)

    owners = batch_order[:, :4]
    own_owners = jnp.sum(jnp.where((jnp.arange(2) == s)[:, None], owners, 0), axis=0)
    wanted = jnp.concatenate([jnp.stack([ri, ri + 1 - 2 * c]).astype(jnp.int32), own_owners])
    all_places = jnp.arange(tiles.shape[0], dtype=jnp.int32)
    found = jnp.sum(jnp.where(wanted[:, None] == all_places[None, :], tiles[None, :], 0), axis=1)
    mine = jnp.arange(4, dtype=jnp.int32) == 2 * h + c
    my_tile = jnp.sum(jnp.where(mine, found[2:], 0)).reshape(1)
    ds, dh = jnp.array([0, 0, 1, 1] * 2), jnp.array([0, 1, 0, 1] * 2)
    to_core = jnp.array([1] * 4 + [0] * 4)
    flow = (s ^ ds) * 4 + (h ^ dh) * 2 + (c ^ to_core)
    flow_owner = jnp.sum(
        jnp.where(flow[:, None] == jnp.arange(8)[None, :], owners.reshape(1, -1), 0), axis=1
    ).astype(jnp.int32)
    table = flow_owner // NC
    here_now = (flow_owner[4:] % NC == c)[:, None, None, None]

    own_x = dielectric[0]
    ring = [(i, (i + 1) % (CHIPS * NC)) for i in range(CHIPS * NC)]
    back = [(j, i) for i, j in ring]
    before = lax.ppermute(own_x, ("z", "x", "core"), ring)
    behind = lax.ppermute(own_x, ("z", "x", "core"), back)
    g_other = shift(greens[0], "ao", 1)
    mask_full = jnp.repeat(jnp.repeat(band_mask, 64, axis=0), 64, axis=1).astype(BF)
    band = coulomb_band * mask_full
    stacked = jnp.concatenate([before, own_x, behind], axis=0)
    wt = lax.dot_general(stacked, band, (((0,), (1,)), ((), ())), preferred_element_type=F32).astype(BF)
    wt = wt * keep[None, :]
    wt = wt.reshape(2, rows, rows)
    half_rows = rows // 2
    q = half_rows // CHIPS
    wt_own = jnp.where(c == 0, wt[0], wt[1])
    wt_oth = shift(jnp.where(c == 0, wt[1], wt[0]), "core", 1)
    g2 = g_pairs(
        greens[0], g_other, jnp.concatenate([found[:2], my_tile, h.reshape(1)]).astype(jnp.int32), width
    )

    m_core = after(shift(three_centre, "core", 1), g_other)
    m_both = lax.ppermute(m_core, ("sec", "core", "ao"), along_y())

    send = after(masked_rows(three_centre, h, centre_mask), before, behind)
    spread = lax.all_to_all(send, ("z", "x"), 0, 0, tiled=True).reshape(CHIPS, q, mus, width)
    picked = pick(spread, table, 8, (m_both,))
    m_both = after(m_both, picked)
    m_sec = shift(m_both, "core", 1)
    ys_0 = y_part(None, 0, after(wt_own, picked), g2, three_centre)
    given = shift(picked[:4], "core", 1)
    pieces = jnp.where(here_now, picked[4:], given)
    got = [
        pieces[0],
        shift(pieces[1], "ao", 1),
        shift(pieces[2], "sec", 1),
        lax.ppermute(pieces[3], ("sec", "ao"), [(i, 3 - i) for i in range(4)]),
    ]
    got = jnp.stack(got).reshape(2, 2, q, mus, width)
    got = jnp.where(s == 0, got, got[::-1])
    got = jnp.where(h == 0, got, got[:, ::-1])
    halves = jnp.transpose(got, (1, 2, 0, 3, 4)).reshape(2, q, 2 * mus, width)
    piece_a, piece_b = halves[0], after(halves[1], ys_0)
    ys_1 = y_part(ys_0, 1, wt_oth, g2, m_core)
    ys_2 = y_part(ys_1, 3, wt_oth, g2, m_both)
    ys = y_part(ys_2, 2, wt_own, g2, m_sec)

    rel_z = [0]
    for step in range(1, NZ // 2):
        rel_z += [step, -step]
    rel_z.append(NZ // 2)
    lists = [], [], []

    def ids(first, zs, xs):
        start = len(lists[0])
        for dz in zs:
            for dx in xs:
                for entry, item in zip(lists, (first, dz, dx)):
                    entry.append(item)
        return start

    def ids_a(offset, first, count):
        return ids(0, [offset], list(range(first, first + count)))

    def ids_b(offset, first, count):
        return ids(CHIPS, rel_z[first : first + count], [offset])

    a_ids = {off: ids_a(off, 0, NX) for off in rel_z[:-1]}
    a_ids[4, 0], a_ids[4, 2] = ids_a(4, 0, 2), ids_a(4, 2, 2)
    b_ids = {off: ids_b(off, 0, NZ) for off in (0, 1, -1)}
    b_ids[2, 0], b_ids[2, 4] = ids_b(2, 0, 4), ids_b(2, 4, 4)
    first, off_z, off_x = (jnp.array(entry, jnp.int32) for entry in lists)
    places = first + ((z - off_z) % NZ) * NX + (x - off_x) % NX

    up, down = shift(piece_b, "z", 1), shift(piece_b, "z", -1)
    up, down = after(up, ys_1), after(down, ys_1)
    pieces = [piece_b, up, down]
    piece_a = after(piece_a, up, down)
    chunk_a = jnp.concatenate([piece_a] + [shift(piece_a, "x", d) for d in range(1, NX)], axis=0)
    up, down = shift(up, "z", 1), shift(down, "z", -1)
    up, down = after(up, ys_2), after(down, ys_2)
    pieces += [up, down]
    up, down = shift(up, "z", 1), shift(down, "z", -1)
    pieces += [up, down]
    pieces.append(shift(up, "z", 1))
    chunk_b = jnp.concatenate(pieces, axis=0)
    chunk_a = after(chunk_a, chunk_b)

    up1, down1 = shift(chunk_a, "z", 1), shift(chunk_a, "z", -1)
    up1, down1 = after(up1, ys), after(down1, ys)
    up_b, down_b = shift(chunk_b, "x", 1), shift(chunk_b, "x", -1)
    up2, down2 = shift(up1, "z", 1), shift(down1, "z", -1)
    total = contract(None, ys, places, [(chunk_a, a_ids[0]), (chunk_b, b_ids[0])], q)
    up2, down2 = after(up2, total), after(down2, total)
    up3, down3 = shift(up2, "z", 1), shift(down2, "z", -1)
    total = contract(total, ys, places, [(up1, a_ids[1]), (down1, a_ids[-1]), (up2, a_ids[2]), (down2, a_ids[-2])], q)
    up3, down3 = after(up3, total), after(down3, total)
    part = chunk_a.shape[0] // 2
    last_up, last_down = shift(up3[:part], "z", 1), shift(down3[part:], "z", -1)
    part_b = chunk_b.shape[0] // 2
    last_up_b, last_down_b = shift(up_b[:part_b], "x", 1), shift(down_b[part_b:], "x", -1)
    total = contract(
        total,
        ys,
        places,
        [
            (up3, a_ids[3]),
            (down3, a_ids[-3]),
            (up_b, b_ids[1]),
            (down_b, b_ids[-1]),
            (last_up_b, b_ids[2, 0]),
            (last_down_b, b_ids[2, 4]),
        ],
        q,
    )
    total = contract(total, ys, places, [(last_up, a_ids[4, 0]), (last_down, a_ids[4, 2])], q)

    row_places = jnp.arange(8, dtype=jnp.int32)
    starts = 2 * jnp.concatenate([found[:2], found[:2]]) + jnp.stack([s, s, 1 - s, 1 - s])
    here = starts[:, None] == row_places[None, :]
    partial = jnp.sum(jnp.where(here[:, :, None, None], total.reshape(4, 1, mus, width), 0.0), axis=0)
    partial = partial.reshape(8 * mus, width)
    moved = lax.all_to_all(partial, ("z", "x", "core", "ao"), 0, 0, tiled=True)
    own_rows = partial.shape[0] // (CHIPS * NC * 2)
    summed = jnp.sum(moved.reshape(CHIPS, NC, 2, own_rows, width), axis=0)
    col_places = jnp.arange(4, dtype=jnp.int32)
    there = found[2:].reshape(2, NC).T[:, :, None] == col_places
    out = -jnp.sum(jnp.where(there[:, :, None, :, None], summed[:, :, :, None, :], 0.0), axis=(0, 1))
    return out.reshape(1, own_rows, 4 * width)


def solution(mesh):
    devices = mesh.devices.reshape(2, NZ, NX, NC, 2)
    split = Mesh(devices, ("sec", "z", "x", "core", "ao"))
    ri = ("z", "x", "core")
    placed = (
        P(ri, None),
        P(ri, None),
        P("sec", ri, "ao"),
        P(ri, "sec", None),
        P(ri),
        P("sec", "ao", None),
        P(),
        P(),
    )
    return jax.shard_map(
        body, mesh=split, in_specs=placed, out_specs=P("sec", ri + ("ao",), None), check_vma=False
    )
```

profile of v0, /device:TPU:1, one launch (start us, length us, event | category | flops | bytes accessed | tf_op | source)
XLA Modules:
  0.0 227.5 jit_solution(14474672619683512435)
XLA Ops:
  0.0 3.2 %collective-permute-start.3 = (bf16[256,64,128]{2,1,0:T(8,128)(2,1)}, bf16[256,64,128]{2,1,0:T(8,128)(2,1)}, u32[]{:S(2)}, u32[]{:S(2)}) collective-permute-start(bf16[256,64,128]{2,1,0:T(8,128)(2,1)} %m_ref.1), channel_id=1, source_target_pairs={{0,2},{2,0},{1,3},{3,1},{4,6},{6,4},{5,7},{7,5},{8,10},{10,8},{9,1... | collective-permute-start | bytes 12582920 | tf_op jit(solution)/shard_map/ppermute | solution.py:17
  5.8 7.1 %collective-permute-done.2.oth_ref.refs_1_ = bf16[256,512]{1,0:T(8,128)(2,1)S(1)} collective-permute-done((bf16[256,512]{1,0:T(8,128)(2,1)}, bf16[256,512]{1,0:T(8,128)(2,1)S(1)}, u32[]{:S(2)}, u32[]{:S(2)}) %collective-permute-start.2) | collective-permute-done | bytes 262176 | tf_op jit(solution)/shard_map/ppermute | solution.py:17
  15.2 3.4 %masked_rows.1.refs_0_ = bf16[128,64,128]{2,1,0:T(8,128)(2,1)} custom-call(s32[5]{0:T(128)} %pad_add_fusion.2.tab_ref, bf16[256,64,128]{2,1,0:T(8,128)(2,1)} %m_ref.1), custom_call_target="tpu_custom_call" | custom-call | flops 1000 | bytes 1000 | tf_op jit(solution)/shard_map/masked_rows/pallas_call | solution.py:190
  20.1 11.0 %all-to-all-start = ((bf16[128,64,128]{2,1,0:T(8,128)(2,1)}), bf16[128,64,128]{2,1,0:T(8,128)(2,1)S(1)}, u32[]{:S(2)}, u32[]{:S(2)}) async-start(bf16[128,64,128]{2,1,0:T(8,128)(2,1)} %after.18), calls=%async_computation | async-start | bytes 4194304 | tf_op jit(solution)/shard_map/all_to_all | solution.py:286
  35.8 45.3 %all-to-all-done = bf16[128,64,128]{2,1,0:T(8,128)(2,1)S(1)} async-done(((bf16[128,64,128]{2,1,0:T(8,128)(2,1)}), bf16[128,64,128]{2,1,0:T(8,128)(2,1)S(1)}, u32[]{:S(2)}, u32[]{:S(2)}) %all-to-all-start) | async-done | bytes 2097184 | tf_op jit(solution)/shard_map/all_to_all | solution.py:286
  82.5 2.7 %pick.1.refs_1_ = bf16[8,4,64,128]{3,2,1,0:T(8,128)(2,1)} custom-call(s32[8]{0:T(128)} %and_select_fusion.1.tab_ref, bf16[32,4,64,128]{3,2,1,0:T(8,128)(2,1)} %bitcast.34, bf16[32,4,64,128]{3,2,1,0:T(8,128)(2,1)} %bitcast.35, bf16[32,4,64,128]{3,2,1,0:T(8,128)(2,1)} %bitcast.36, bf16[32,4,64,128]{3,2,1,0:T(8,128)(2,1)} %bitcast.37, ...), custom_call_target="tpu_custom_call" | custom-call | flops 1000 | bytes 1000 | tf_op jit(solution)/shard_map/pick/pallas_call | solution.py:162
  93.1 3.1 %collective-permute-start.10 = (bf16[4,64,128]{2,1,0:T(8,128)(2,1)S(1)}, bf16[4,64,128]{2,1,0:T(8,128)(2,1)S(1)}, u32[]{:S(2)}, u32[]{:S(2)}) collective-permute-start(bf16[4,64,128]{2,1,0:T(8,128)(2,1)S(1)} %get-tuple-element.8), channel_id=1, source_target_pairs={{0,129},{1,128},{128,1},{129,0},{2,131},{3,130},{130,3},{131,2},{4... | collective-permute-start | bytes 196616 | tf_op jit(solution)/shard_map/ppermute | solution.py:297
  96.2 6.5 %y_part.4.unused.refs_1_ = bf16[256,256,128]{2,1,0:T(8,128)(2,1)} custom-call(bf16[256,256]{1,0:T(8,128)(2,1)} %after.20.wt_ref, bf16[2,256,256]{2,1,0:T(8,128)(2,1)} %g_pairs.1.g_ref.g, bf16[256,64,128]{2,1,0:T(8,128)(2,1)} %m_ref.1), custom_call_target="tpu_custom_call" | custom-call | flops 21474836480 | bytes 167772160 | tf_op jit(solution)/shard_map/y_part/pallas_call | solution.py:61
  103.9 2.4 %collective-permute-start.12 = (bf16[4,128,128]{2,1,0:T(8,128)(2,1)}, bf16[4,128,128]{2,1,0:T(8,128)(2,1)S(1)}, u32[]{:S(2)}, u32[]{:S(2)}) collective-permute-start(bf16[4,128,128]{2,1,0:T(8,128)(2,1)} %after.21), channel_id=1, source_target_pairs={{0,112},{16,0},{32,16},{48,32},{64,48},{80,64},{96,80},{112,96},{1... | collective-permute-start | bytes 393224 | tf_op jit(solution)/shard_map/ppermute | solution.py:17
  107.0 6.5 %y_part.5.unused.refs_1_ = bf16[256,256,128]{2,1,0:T(8,128)(2,1)} custom-call(bf16[256,256]{1,0:T(8,128)(2,1)} %copy-done.41, bf16[2,256,256]{2,1,0:T(8,128)(2,1)} %g_pairs.1.g_ref.g, bf16[256,64,128]{2,1,0:T(8,128)(2,1)} %after.17.m, bf16[256,256,128]{2,1,0:T(8,128)(2,1)} %y_part.4.unused.refs_1_), custom_call_target="tpu_custom_call", output_to_operand_aliasing={{}: (3, {})} | custom-call | flops 21474836480 | bytes 167772160 | tf_op jit(solution)/shard_map/y_part/pallas_call | solution.py:61
  114.9 2.7 %collective-permute-start.17 = (bf16[4,128,128]{2,1,0:T(8,128)(2,1)}, bf16[4,128,128]{2,1,0:T(8,128)(2,1)S(1)}, u32[]{:S(2)}, u32[]{:S(2)}) collective-permute-start(bf16[4,128,128]{2,1,0:T(8,128)(2,1)} %after.23.refs_2_), channel_id=1, source_target_pairs={{0,112},{16,0},{32,16},{48,32},{64,48},{80,64},{96,80},{112,96},{1... | collective-permute-start | bytes 393224 | tf_op jit(solution)/shard_map/ppermute | solution.py:17
  119.8 6.5 %y_part.6.unused.refs_1_ = bf16[256,256,128]{2,1,0:T(8,128)(2,1)} custom-call(bf16[256,256]{1,0:T(8,128)(2,1)} %copy-done.41, bf16[2,256,256]{2,1,0:T(8,128)(2,1)} %g_pairs.1.g_ref.g, bf16[256,64,128]{2,1,0:T(8,128)(2,1)} %after.19.m, bf16[256,256,128]{2,1,0:T(8,128)(2,1)} %y_part.5.unused.refs_1_), custom_call_target="tpu_custom_call", output_to_operand_aliasing={{}: (3, {})} | custom-call | flops 21474836480 | bytes 167772160 | tf_op jit(solution)/shard_map/y_part/pallas_call | solution.py:61
  133.6 5.0 %collective-permute-done.20 = bf16[4,128,128]{2,1,0:T(8,128)(2,1)S(1)} collective-permute-done((bf16[4,128,128]{2,1,0:T(8,128)(2,1)S(1)}, bf16[4,128,128]{2,1,0:T(8,128)(2,1)S(1)}, u32[]{:S(2)}, u32[]{:S(2)}) %collective-permute-start.20) | collective-permute-done | bytes 131104 | tf_op jit(solution)/shard_map/ppermute | solution.py:17
  141.0 2.7 %collective-permute-start.30 = (bf16[32,128,128]{2,1,0:T(8,128)(2,1)}, bf16[32,128,128]{2,1,0:T(8,128)(2,1)S(1)}, u32[]{:S(2)}, u32[]{:S(2)}) collective-permute-start(bf16[32,128,128]{2,1,0:T(8,128)(2,1)} %copy-done.2), channel_id=1, source_target_pairs={{0,12},{4,0},{8,4},{12,8},{1,13},{5,1},{9,5},{13,9},{2,14},{6,2},{... | collective-permute-start | bytes 3145736 | tf_op jit(solution)/shard_map/ppermute | solution.py:17
  143.7 6.6 %y_part.7.refs_1_.refs_2_.refs_3_.refs_4_.refs_5_.refs_6_.refs_7_.refs_8_.refs_9_.refs_10_.refs_11_.refs_12_.refs_13_.refs_14_.refs_15_.refs_16_ = bf16[256,256,128]{2,1,0:T(8,128)(2,1)} custom-call(bf16[256,256]{1,0:T(8,128)(2,1)} %copy-done.22, bf16[2,256,256]{2,1,0:T(8,128)(2,1)} %g_pairs.1.g_ref.g, ...), custom_call_target="tpu_custom_call", output_to_operand_aliasing={{}: (3, {})} | custom-call | flops 21474836480 | bytes 167772160 | tf_op jit(solution)/shard_map/y_part/pallas_call | solution.py:61
  154.0 4.2 %contract.4.refs_1_.refs_13_ = f32[256,128]{1,0:T(8,128)} custom-call(s32[64]{0:T(128)} %fusion.7.refs_0_, bf16[256,256,128]{2,1,0:T(8,128)(2,1)} %y_part.7.refs_1_.refs_2_.refs_3_.refs_4_.refs_5_.refs_6_.refs_7_.refs_8_.refs_9_.refs_10_.refs_11_.refs_12_.refs_13_.refs_14_.refs_15_.refs_16_, ...), custom_call_target="tpu_custom_call" | custom-call | flops 402653184 | bytes 4718592 | tf_op jit(solution)/shard_map/contract/pallas_call | solution.py:132
  160.5 2.4 %collective-permute-start.27 = (bf16[16,128,128]{2,1,0:T(8,128)(2,1)}, bf16[16,128,128]{2,1,0:T(8,128)(2,1)S(1)}, u32[]{:S(2)}, u32[]{:S(2)}) collective-permute-start(bf16[16,128,128]{2,1,0:T(8,128)(2,1)} %after.31.refs_12_), channel_id=1, source_target_pairs={{0,112},{16,0},{32,16},{48,32},{64,48},{80,64},{96,80},{112,96},{1... | collective-permute-start | bytes 1572872 | tf_op jit(solution)/shard_map/ppermute | solution.py:17
  165.6 2.7 %collective-permute-start.32 = (bf16[16,128,128]{2,1,0:T(8,128)(2,1)}, bf16[16,128,128]{2,1,0:T(8,128)(2,1)}, u32[]{:S(2)}, u32[]{:S(2)}) collective-permute-start(bf16[16,128,128]{2,1,0:T(8,128)(2,1)} %slice.102), channel_id=1, source_target_pairs={{0,12},{4,0},{8,4},{12,8},{1,13},{5,1},{9,5},{13,9},{2,14},{6,2},{... | collective-permute-start | bytes 1572872 | tf_op jit(solution)/shard_map/ppermute | solution.py:17
  168.3 4.9 %contract.5.refs_1_.refs_23_ = f32[256,128]{1,0:T(8,128)} custom-call(s32[64]{0:T(128)} %fusion.7.refs_0_, bf16[256,256,128]{2,1,0:T(8,128)(2,1)} %y_part.7.refs_1_.refs_2_.refs_3_.refs_4_.refs_5_.refs_6_.refs_7_.refs_8_.refs_9_.refs_10_.refs_11_.refs_12_.refs_13_.refs_14_.refs_15_.refs_16_, ...), custom_call_target="tpu_custom_call" | custom-call | flops 536870912 | bytes 6291456 | tf_op jit(solution)/shard_map/contract/pallas_call | solution.py:132
  175.0 2.7 %collective-permute-start.28 = (bf16[8,128,128]{2,1,0:T(8,128)(2,1)S(1)}, bf16[8,128,128]{2,1,0:T(8,128)(2,1)S(1)}, u32[]{:S(2)}, u32[]{:S(2)}) collective-permute-start(bf16[8,128,128]{2,1,0:T(8,128)(2,1)S(1)} %slice.100), channel_id=1, source_target_pairs={{0,112},{16,0},{32,16},{48,32},{64,48},{80,64},{96,80},{112,96},{1... | collective-permute-start | bytes 786440 | tf_op jit(solution)/shard_map/ppermute | solution.py:17
  180.5 7.4 %contract.6.refs_5_ = f32[256,128]{1,0:T(8,128)} custom-call(s32[64]{0:T(128)} %fusion.7.refs_0_, bf16[256,256,128]{2,1,0:T(8,128)(2,1)} %y_part.7.refs_1_.refs_2_.refs_3_.refs_4_.refs_5_.refs_6_.refs_7_.refs_8_.refs_9_.refs_10_.refs_11_.refs_12_.refs_13_.refs_14_.refs_15_.refs_16_, ...), custom_call_target="tpu_custom_call" | custom-call | flops 1073741824 | bytes 12582912 | tf_op jit(solution)/shard_map/contract/pallas_call | solution.py:132
  189.3 3.2 %contract.7 = f32[256,128]{1,0:T(8,128)} custom-call(s32[64]{0:T(128)} %fusion.7.refs_0_, bf16[256,256,128]{2,1,0:T(8,128)(2,1)} %y_part.7.refs_1_.refs_2_.refs_3_.refs_4_.refs_5_.refs_6_.refs_7_.refs_8_.refs_9_.refs_10_.refs_11_.refs_12_.refs_13_.refs_14_.refs_15_.refs_16_, ...), custom_call_target="tpu_custom_call" | custom-call | flops 134217728 | bytes 1572864 | tf_op jit(solution)/shard_map/contract/pallas_call | solution.py:132
  194.3 16.7 %all-to-all-start.1 = ((f32[128,4,128]{2,1,0:T(4,128)}), f32[128,4,128]{2,1,0:T(4,128)S(1)}, u32[]{:S(2)}, u32[]{:S(2)}) async-start(f32[128,4,128]{2,1,0:T(4,128)} %bitcast.23), calls=%async_computation.1 | async-start | bytes 524288 | tf_op jit(solution)/shard_map/all_to_all | solution.py:383
  211.3 15.4 %all-to-all-done.1 = f32[128,4,128]{2,1,0:T(4,128)S(1)} async-done(((f32[128,4,128]{2,1,0:T(4,128)}), f32[128,4,128]{2,1,0:T(4,128)S(1)}, u32[]{:S(2)}, u32[]{:S(2)}) %all-to-all-start.1) | async-done | bytes 262176 | tf_op jit(solution)/shard_map/all_to_all | solution.py:383
  (217 shorter events, 52.4 us)
Async XLA Ops:
  0.0 12.9 %collective-permute-start.3 = (bf16[256,64,128]{2,1,0:T(8,128)(2,1)}, bf16[256,64,128]{2,1,0:T(8,128)(2,1)}, u32[]{:S(2)}, u32[]{:S(2)}) collective-permute-start(bf16[256,64,128]{2,1,0:T(8,128)(2,1)} %m_ref.1), channel_id=1, source_target_pairs={{0,2},{2,0},{1,3},{3,1},{4,6},{6,4},{5,7},{7,5},{8,10},{10,8},{9,1... | collective-permute-start | bytes 12582920 | tf_op jit(solution)/shard_map/ppermute | solution.py:17
  4.4 14.2 %collective-permute-start = (bf16[256,512]{1,0:T(8,128)(2,1)}, bf16[256,512]{1,0:T(8,128)(2,1)S(1)}, u32[]{:S(2)}, u32[]{:S(2)}) collective-permute-start(bf16[256,512]{1,0:T(8,128)(2,1)} %bitcast.54), channel_id=1, source_target_pairs={{0,2},{2,4},{4,6},{6,8},{8,10},{10,12},{12,14},{14,16},{16,18},{18... | collective-permute-start | bytes 786440 | tf_op jit(solution)/shard_map/ppermute | solution.py:265
  5.8 12.9 %collective-permute-start.1 = (bf16[256,512]{1,0:T(8,128)(2,1)}, bf16[256,512]{1,0:T(8,128)(2,1)S(1)}, u32[]{:S(2)}, u32[]{:S(2)}) collective-permute-start(bf16[256,512]{1,0:T(8,128)(2,1)} %bitcast.55), channel_id=1, source_target_pairs={{2,0},{4,2},{6,4},{8,6},{10,8},{12,10},{14,12},{16,14},{18,16},{20... | collective-permute-start | bytes 786440 | tf_op jit(solution)/shard_map/ppermute | solution.py:266
  13.6 67.5 %collective-permute-start.4 = (bf16[256,64,128]{2,1,0:T(8,128)(2,1)}, bf16[256,64,128]{2,1,0:T(8,128)(2,1)}, u32[]{:S(2)}, u32[]{:S(2)}) collective-permute-start(bf16[256,64,128]{2,1,0:T(8,128)(2,1)} %after.17.m), channel_id=1, source_target_pairs={{0,128},{2,131},{128,1},{130,2},{1,129},{3,130},{129,0},{131,3},{4... | collective-permute-start | bytes 12582920 | tf_op jit(solution)/shard_map/ppermute | solution.py:283
  20.1 61.1 %all-to-all-start = ((bf16[128,64,128]{2,1,0:T(8,128)(2,1)}), bf16[128,64,128]{2,1,0:T(8,128)(2,1)S(1)}, u32[]{:S(2)}, u32[]{:S(2)}) async-start(bf16[128,64,128]{2,1,0:T(8,128)(2,1)} %after.18), calls=%async_computation | async-start | bytes 4194304 | tf_op jit(solution)/shard_map/all_to_all | solution.py:286
  88.7 17.7 %collective-permute-start.6 = (bf16[256,256]{1,0:T(8,128)(2,1)S(1)}, bf16[256,256]{1,0:T(8,128)(2,1)S(1)}, u32[]{:S(2)}, u32[]{:S(2)}) collective-permute-start(bf16[256,256]{1,0:T(8,128)(2,1)S(1)} %get-tuple-element.11), channel_id=1, source_target_pairs={{0,2},{2,0},{1,3},{3,1},{4,6},{6,4},{5,7},{7,5},{8,10},{10,8},{9,1... | collective-permute-start | bytes 393224 | tf_op jit(solution)/shard_map/ppermute | solution.py:17
  91.7 52.0 %collective-permute-start.5 = (bf16[256,64,128]{2,1,0:T(8,128)(2,1)}, bf16[256,64,128]{2,1,0:T(8,128)(2,1)}, u32[]{:S(2)}, u32[]{:S(2)}) collective-permute-start(bf16[256,64,128]{2,1,0:T(8,128)(2,1)} %after.19.m), channel_id=1, source_target_pairs={{0,2},{2,0},{1,3},{3,1},{4,6},{6,4},{5,7},{7,5},{8,10},{10,8},{9,1... | collective-permute-start | bytes 12582920 | tf_op jit(solution)/shard_map/ppermute | solution.py:17
  92.8 9.9 %collective-permute-start.8 = (bf16[4,64,128]{2,1,0:T(8,128)(2,1)S(1)}, bf16[4,64,128]{2,1,0:T(8,128)(2,1)S(1)}, u32[]{:S(2)}, u32[]{:S(2)}) collective-permute-start(bf16[4,64,128]{2,1,0:T(8,128)(2,1)S(1)} %get-tuple-element.10), channel_id=1, source_target_pairs={{0,1},{1,0},{2,3},{3,2},{4,5},{5,4},{6,7},{7,6},{8,9},{9,8},{10,11... | collective-permute-start | bytes 196616 | tf_op jit(solution)/shard_map/ppermute | solution.py:17
  103.7 9.9 %collective-permute-start.11 = (bf16[4,128,128]{2,1,0:T(8,128)(2,1)}, bf16[4,128,128]{2,1,0:T(8,128)(2,1)S(1)}, u32[]{:S(2)}, u32[]{:S(2)}) collective-permute-start(bf16[4,128,128]{2,1,0:T(8,128)(2,1)} %after.21), channel_id=1, source_target_pairs={{0,16},{16,32},{32,48},{48,64},{64,80},{80,96},{96,112},{112,0},{1... | collective-permute-start | bytes 393224 | tf_op jit(solution)/shard_map/ppermute | solution.py:17
  103.9 10.3 %collective-permute-start.12 = (bf16[4,128,128]{2,1,0:T(8,128)(2,1)}, bf16[4,128,128]{2,1,0:T(8,128)(2,1)S(1)}, u32[]{:S(2)}, u32[]{:S(2)}) collective-permute-start(bf16[4,128,128]{2,1,0:T(8,128)(2,1)} %after.21), channel_id=1, source_target_pairs={{0,112},{16,0},{32,16},{48,32},{64,48},{80,64},{96,80},{112,96},{1... | collective-permute-start | bytes 393224 | tf_op jit(solution)/shard_map/ppermute | solution.py:17
  114.2 12.1 %collective-permute-start.16 = (bf16[4,128,128]{2,1,0:T(8,128)(2,1)}, bf16[4,128,128]{2,1,0:T(8,128)(2,1)S(1)}, u32[]{:S(2)}, u32[]{:S(2)}) collective-permute-start(bf16[4,128,128]{2,1,0:T(8,128)(2,1)} %after.22.refs_1_), channel_id=1, source_target_pairs={{0,16},{16,32},{32,48},{48,64},{64,80},{80,96},{96,112},{112,0},{1... | collective-permute-start | bytes 393224 | tf_op jit(solution)/shard_map/ppermute | solution.py:17
  114.9 13.3 %collective-permute-start.17 = (bf16[4,128,128]{2,1,0:T(8,128)(2,1)}, bf16[4,128,128]{2,1,0:T(8,128)(2,1)S(1)}, u32[]{:S(2)}, u32[]{:S(2)}) collective-permute-start(bf16[4,128,128]{2,1,0:T(8,128)(2,1)} %after.23.refs_2_), channel_id=1, source_target_pairs={{0,112},{16,0},{32,16},{48,32},{64,48},{80,64},{96,80},{112,96},{1... | collective-permute-start | bytes 393224 | tf_op jit(solution)/shard_map/ppermute | solution.py:17
  117.6 11.3 %collective-permute-start.13 = (bf16[4,128,128]{2,1,0:T(8,128)(2,1)}, bf16[4,128,128]{2,1,0:T(8,128)(2,1)S(1)}, u32[]{:S(2)}, u32[]{:S(2)}) collective-permute-start(bf16[4,128,128]{2,1,0:T(8,128)(2,1)} %after.24), channel_id=1, source_target_pairs={{0,4},{4,8},{8,12},{12,0},{1,5},{5,9},{9,13},{13,1},{2,6},{6,10},{... | collective-permute-start | bytes 393224 | tf_op jit(solution)/shard_map/ppermute | solution.py:17
  119.0 12.0 %collective-permute-start.14 = (bf16[4,128,128]{2,1,0:T(8,128)(2,1)}, bf16[4,128,128]{2,1,0:T(8,128)(2,1)S(1)}, u32[]{:S(2)}, u32[]{:S(2)}) collective-permute-start(bf16[4,128,128]{2,1,0:T(8,128)(2,1)} %after.24), channel_id=1, source_target_pairs={{0,8},{4,12},{8,0},{12,4},{1,9},{5,13},{9,1},{13,5},{2,10},{6,14},... | collective-permute-start | bytes 393224 | tf_op jit(solution)/shard_map/ppermute | solution.py:17
  139.6 10.7 %collective-permute-start.24 = (bf16[16,128,128]{2,1,0:T(8,128)(2,1)}, bf16[16,128,128]{2,1,0:T(8,128)(2,1)S(1)}, u32[]{:S(2)}, u32[]{:S(2)}) collective-permute-start(bf16[16,128,128]{2,1,0:T(8,128)(2,1)} %after.27.refs_7_), channel_id=1, source_target_pairs={{0,112},{16,0},{32,16},{48,32},{64,48},{80,64},{96,80},{112,96},{1... | collective-permute-start | bytes 1572872 | tf_op jit(solution)/shard_map/ppermute | solution.py:17
  139.6 12.8 %collective-permute-start.21 = (bf16[16,128,128]{2,1,0:T(8,128)(2,1)}, bf16[16,128,128]{2,1,0:T(8,128)(2,1)S(1)}, u32[]{:S(2)}, u32[]{:S(2)}) collective-permute-start(bf16[16,128,128]{2,1,0:T(8,128)(2,1)} %after.27.refs_7_), channel_id=1, source_target_pairs={{0,16},{16,32},{32,48},{48,64},{64,80},{80,96},{96,112},{112,0},{1... | collective-permute-start | bytes 1572872 | tf_op jit(solution)/shard_map/ppermute | solution.py:17
  141.0 22.8 %collective-permute-start.29 = (bf16[32,128,128]{2,1,0:T(8,128)(2,1)}, bf16[32,128,128]{2,1,0:T(8,128)(2,1)S(1)}, u32[]{:S(2)}, u32[]{:S(2)}) collective-permute-start(bf16[32,128,128]{2,1,0:T(8,128)(2,1)} %copy-done.2), channel_id=1, source_target_pairs={{0,4},{4,8},{8,12},{12,0},{1,5},{5,9},{9,13},{13,1},{2,6},{6,10},{... | collective-permute-start | bytes 3145736 | tf_op jit(solution)/shard_map/ppermute | solution.py:17
  141.0 23.7 %collective-permute-start.30 = (bf16[32,128,128]{2,1,0:T(8,128)(2,1)}, bf16[32,128,128]{2,1,0:T(8,128)(2,1)S(1)}, u32[]{:S(2)}, u32[]{:S(2)}) collective-permute-start(bf16[32,128,128]{2,1,0:T(8,128)(2,1)} %copy-done.2), channel_id=1, source_target_pairs={{0,12},{4,0},{8,4},{12,8},{1,13},{5,1},{9,5},{13,9},{2,14},{6,2},{... | collective-permute-start | bytes 3145736 | tf_op jit(solution)/shard_map/ppermute | solution.py:17
  160.5 12.7 %collective-permute-start.27 = (bf16[16,128,128]{2,1,0:T(8,128)(2,1)}, bf16[16,128,128]{2,1,0:T(8,128)(2,1)S(1)}, u32[]{:S(2)}, u32[]{:S(2)}) collective-permute-start(bf16[16,128,128]{2,1,0:T(8,128)(2,1)} %after.31.refs_12_), channel_id=1, source_target_pairs={{0,112},{16,0},{32,16},{48,32},{64,48},{80,64},{96,80},{112,96},{1... | collective-permute-start | bytes 1572872 | tf_op jit(solution)/shard_map/ppermute | solution.py:17
  163.8 14.0 %collective-permute-start.23 = (bf16[16,128,128]{2,1,0:T(8,128)(2,1)}, bf16[16,128,128]{2,1,0:T(8,128)(2,1)S(1)}, u32[]{:S(2)}, u32[]{:S(2)}) collective-permute-start(bf16[16,128,128]{2,1,0:T(8,128)(2,1)} %after.29.refs_11_), channel_id=1, source_target_pairs={{0,16},{16,32},{32,48},{48,64},{64,80},{80,96},{96,112},{112,0},{1... | collective-permute-start | bytes 1572872 | tf_op jit(solution)/shard_map/ppermute | solution.py:17
  164.7 15.0 %collective-permute-start.31 = (bf16[16,128,128]{2,1,0:T(8,128)(2,1)}, bf16[16,128,128]{2,1,0:T(8,128)(2,1)S(1)}, u32[]{:S(2)}, u32[]{:S(2)}) collective-permute-start(bf16[16,128,128]{2,1,0:T(8,128)(2,1)} %slice.101), channel_id=1, source_target_pairs={{0,4},{4,8},{8,12},{12,0},{1,5},{5,9},{9,13},{13,1},{2,6},{6,10},{... | collective-permute-start | bytes 1572872 | tf_op jit(solution)/shard_map/ppermute | solution.py:17
  165.6 14.1 %collective-permute-start.32 = (bf16[16,128,128]{2,1,0:T(8,128)(2,1)}, bf16[16,128,128]{2,1,0:T(8,128)(2,1)}, u32[]{:S(2)}, u32[]{:S(2)}) collective-permute-start(bf16[16,128,128]{2,1,0:T(8,128)(2,1)} %slice.102), channel_id=1, source_target_pairs={{0,12},{4,0},{8,4},{12,8},{1,13},{5,1},{9,5},{13,9},{2,14},{6,2},{... | collective-permute-start | bytes 1572872 | tf_op jit(solution)/shard_map/ppermute | solution.py:17
  175.0 12.9 %collective-permute-start.28 = (bf16[8,128,128]{2,1,0:T(8,128)(2,1)S(1)}, bf16[8,128,128]{2,1,0:T(8,128)(2,1)S(1)}, u32[]{:S(2)}, u32[]{:S(2)}) collective-permute-start(bf16[8,128,128]{2,1,0:T(8,128)(2,1)S(1)} %slice.100), channel_id=1, source_target_pairs={{0,112},{16,0},{32,16},{48,32},{64,48},{80,64},{96,80},{112,96},{1... | collective-permute-start | bytes 786440 | tf_op jit(solution)/shard_map/ppermute | solution.py:17
  194.3 32.4 %all-to-all-start.1 = ((f32[128,4,128]{2,1,0:T(4,128)}), f32[128,4,128]{2,1,0:T(4,128)S(1)}, u32[]{:S(2)}, u32[]{:S(2)}) async-start(f32[128,4,128]{2,1,0:T(4,128)} %bitcast.23), calls=%async_computation.1 | async-start | bytes 524288 | tf_op jit(solution)/shard_map/all_to_all | solution.py:383
  (55 other events, 335.5 us)
where the time goes:
time: 228 us; the launch traced here: 227 us
  waiting for transfers between devices  75.1 us (33%)
  starting transfers between devices  65.7 us (29%)
  Pallas kernels  54.2 us (24%)
  local copies, waits for them, and re-layouts  23.2 us (10%)
  other arithmetic  8.23 us (4%)
    all_to_all x1, waiting for transfers between devices, body(): lax.all_to_all(send, ('z', 'x'), 0, 0, tiled=True)  45.3 us
    ppermute x29, starting transfers between devices, shift(): return lax.ppermute(value, axis, [(i, (i + by) % n) for i in range(n)])  32.5 us
    pallas_call x4, Pallas kernels, y_part(): pl.pallas_call(kernel, grid=(steps,), in_specs=specs, out_specs=pl.BlockS...  26.1 us
    pallas_call x4, Pallas kernels, contract(): pl.pallas_call(lambda *refs: contract_kernel(counts, before is not None,...  19.8 us
    all_to_all x1, starting transfers between devices, body(): moved = lax.all_to_all(partial, ('z', 'x', 'core', 'ao'), 0, 0, tiled=True)  16.7 us
    unnamed x97, local copies, waits for them, and re-layouts  16.4 us
    all_to_all x1, waiting for transfers between devices, body(): moved = lax.all_to_all(partial, ('z', 'x', 'core', 'ao'), 0, 0, tiled=True)  15.4 us
    ppermute x29, waiting for transfers between devices, shift(): return lax.ppermute(value, axis, [(i, (i + by) % n) for i in range(n)])  14.3 us
  transfers between devices with their start and end apart: 35, of which 6 were waited for; matrix products, arithmetic and copies ran while one was open for 6% of the time, Pallas kernels for 21%

commit v1 on v0

--- a/solution.py
+++ b/solution.py
@@ -7,7 +7,7 @@
 
 NZ, NX, NC = 8, 4, 2
 CHIPS = NZ * NX
-VMEM = 60 << 20
+VMEM = 52 << 20
 BF = jnp.bfloat16
 F32 = jnp.float32
 
@@ -259,7 +259,8 @@
     table = flow_owner // NC
     here_now = (flow_owner[4:] % NC == c)[:, None, None, None]
 
-    own_x = dielectric[0]
+    send = masked_rows(three_centre, h, centre_mask)
+    own_x = after(dielectric[0], send)
     ring = [(i, (i + 1) % (CHIPS * NC)) for i in range(CHIPS * NC)]
     back = [(j, i) for i, j in ring]
     before = lax.ppermute(own_x, ("z", "x", "core"), ring)
@@ -282,7 +283,7 @@
     m_core = after(shift(three_centre, "core", 1), g_other)
     m_both = lax.ppermute(m_core, ("sec", "core", "ao"), along_y())
 
-    send = after(masked_rows(three_centre, h, centre_mask), before, behind)
+    send = after(send, before, behind)
     spread = lax.all_to_all(send, ("z", "x"), 0, 0, tiled=True).reshape(CHIPS, q, mus, width)
     picked = pick(spread, table, 8, (m_both,))
     m_both = after(m_both, picked)
@@ -338,7 +339,6 @@
     piece_a = after(piece_a, up, down)
     chunk_a = jnp.concatenate([piece_a] + [shift(piece_a, "x", d) for d in range(1, NX)], axis=0)
     up, down = shift(up, "z", 1), shift(down, "z", -1)
-    up, down = after(up, ys_2), after(down, ys_2)
     pieces += [up, down]
     up, down = shift(up, "z", 1), shift(down, "z", -1)
     pieces += [up, down]
@@ -347,13 +347,21 @@
     chunk_a = after(chunk_a, chunk_b)
 
     up1, down1 = shift(chunk_a, "z", 1), shift(chunk_a, "z", -1)
-    up1, down1 = after(up1, ys), after(down1, ys)
+    up1, down1 = after(up1, ys_2), after(down1, ys_2)
     up_b, down_b = shift(chunk_b, "x", 1), shift(chunk_b, "x", -1)
     up2, down2 = shift(up1, "z", 1), shift(down1, "z", -1)
-    total = contract(None, ys, places, [(chunk_a, a_ids[0]), (chunk_b, b_ids[0])], q)
-    up2, down2 = after(up2, total), after(down2, total)
+    up2, down2 = after(up2, ys), after(down2, ys)
     up3, down3 = shift(up2, "z", 1), shift(down2, "z", -1)
-    total = contract(total, ys, places, [(up1, a_ids[1]), (down1, a_ids[-1]), (up2, a_ids[2]), (down2, a_ids[-2])], q)
+    total = contract(
+        None,
+        ys,
+        places,
+        [
+            (chunk_a, a_ids[0]),
+            (chunk_b, b_ids[0]),
+        ],
+        q,
+    )
     up3, down3 = after(up3, total), after(down3, total)
     part = chunk_a.shape[0] // 2
     last_up, last_down = shift(up3[:part], "z", 1), shift(down3[part:], "z", -1)
@@ -364,6 +372,10 @@
         ys,
         places,
         [
+            (up1, a_ids[1]),
+            (down1, a_ids[-1]),
+            (up2, a_ids[2]),
+            (down2, a_ids[-2]),
             (up3, a_ids[3]),
             (down3, a_ids[-3]),
             (up_b, b_ids[1]),

time: 228 us -> 208 us (0.912)
  local copies, waits for them, and re-layouts: 23.2 us -> 8.56 us
  Pallas kernels: 54.2 us -> 46.1 us
  other arithmetic: 8.23 us -> 10.6 us
    unnamed x97 -> x46, local copies, waits for them, and re-layouts: 16.4 us -> 5.29 us
    all_to_all x1, waiting for transfers between devices: 45.3 us -> 36.8 us  [body(): lax.all_to_all(send, ('z', 'x'), 0, 0, tiled=True)]
    ppermute x29, waiting for transfers between devices: 14.3 us -> 20 us  [shift(): return lax.ppermute(value, axis, [(i, (i + by) % n) for i in range(n)])]
    pallas_call x4 -> x3, Pallas kernels: 19.8 us -> 14.3 us  [contract(): pl.pallas_call(lambda *refs: contract_kernel(counts, before is not None,...]
  transfers between devices with their start and end apart: 35 -> 35, of which waited for: 6 -> 11; matrix products, arithmetic and copies ran while one was open for 6% -> 7% of each run, Pallas kernels for 21% -> 20%
where the time goes in v1:
time: 208 us; the launch traced here: 207 us
  waiting for transfers between devices  73.9 us (36%)
  starting transfers between devices  67.4 us (32%)
  Pallas kernels  46.1 us (22%)
  other arithmetic  10.6 us (5%)
  local copies, waits for them, and re-layouts  8.56 us (4%)
    all_to_all x1, waiting for transfers between devices, body(): lax.all_to_all(send, ('z', 'x'), 0, 0, tiled=True)  36.8 us
    ppermute x29, starting transfers between devices, shift(): return lax.ppermute(value, axis, [(i, (i + by) % n) for i in range(n)])  34.3 us
    pallas_call x4, Pallas kernels, y_part(): pl.pallas_call(kernel, grid=(steps,), in_specs=specs, out_specs=pl.BlockS...  26 us
    ppermute x29, waiting for transfers between devices, shift(): return lax.ppermute(value, axis, [(i, (i + by) % n) for i in range(n)])  20 us
    all_to_all x1, starting transfers between devices, body(): moved = lax.all_to_all(partial, ('z', 'x', 'core', 'ao'), 0, 0, tiled=True)  15.6 us
    all_to_all x1, waiting for transfers between devices, body(): moved = lax.all_to_all(partial, ('z', 'x', 'core', 'ao'), 0, 0, tiled=True)  15.4 us
    pallas_call x3, Pallas kernels, contract(): pl.pallas_call(lambda *refs: contract_kernel(counts, before is not None,...  14.3 us
    all_to_all x1, starting transfers between devices, body(): lax.all_to_all(send, ('z', 'x'), 0, 0, tiled=True)  13.1 us
  transfers between devices with their start and end apart: 35, of which 11 were waited for; matrix products, arithmetic and copies ran while one was open for 7% of the time, Pallas kernels for 20%

profile of v1, /device:TPU:1, one launch (start us, length us, event | category | flops | bytes accessed | tf_op | source)
XLA Modules:
  0.0 207.5 jit_solution(17452886934498274003)
XLA Ops:
  1.0 3.2 %collective-permute-start.3 = (bf16[256,64,128]{2,1,0:T(8,128)(2,1)}, bf16[256,64,128]{2,1,0:T(8,128)(2,1)}, u32[]{:S(2)}, u32[]{:S(2)}) collective-permute-start(bf16[256,64,128]{2,1,0:T(8,128)(2,1)} %m_ref.1), channel_id=1, source_target_pairs={{0,2},{2,0},{1,3},{3,1},{4,6},{6,4},{5,7},{7,5},{8,10},{10,8},{9,1... | collective-permute-start | bytes 12582920 | tf_op jit(solution)/shard_map/ppermute | solution.py:17
  6.1 3.3 %masked_rows.1.refs_1_.refs_0_ = bf16[128,64,128]{2,1,0:T(8,128)(2,1)} custom-call(s32[5]{0:T(128)S(1)} %pad_add_fusion.1.tab_ref, bf16[256,64,128]{2,1,0:T(8,128)(2,1)} %m_ref.1), custom_call_target="tpu_custom_call" | custom-call | flops 1000 | bytes 1000 | tf_op jit(solution)/shard_map/masked_rows/pallas_call | solution.py:190
  10.8 3.0 %collective-permute-done.2.oth_ref.refs_1_ = bf16[256,512]{1,0:T(8,128)(2,1)S(1)} collective-permute-done((bf16[256,512]{1,0:T(8,128)(2,1)}, bf16[256,512]{1,0:T(8,128)(2,1)S(1)}, u32[]{:S(2)}, u32[]{:S(2)}) %collective-permute-start.2) | collective-permute-done | bytes 262176 | tf_op jit(solution)/shard_map/ppermute | solution.py:17
  16.6 13.1 %all-to-all-start = ((bf16[128,64,128]{2,1,0:T(8,128)(2,1)}), bf16[128,64,128]{2,1,0:T(8,128)(2,1)S(1)}, u32[]{:S(2)}, u32[]{:S(2)}) async-start(bf16[128,64,128]{2,1,0:T(8,128)(2,1)} %after.18), calls=%async_computation | async-start | bytes 4194304 | tf_op jit(solution)/shard_map/all_to_all | solution.py:287
  41.5 36.8 %all-to-all-done = bf16[128,64,128]{2,1,0:T(8,128)(2,1)S(1)} async-done(((bf16[128,64,128]{2,1,0:T(8,128)(2,1)}), bf16[128,64,128]{2,1,0:T(8,128)(2,1)S(1)}, u32[]{:S(2)}, u32[]{:S(2)}) %all-to-all-start) | async-done | bytes 2097184 | tf_op jit(solution)/shard_map/all_to_all | solution.py:287
  85.0 1.9 collective-permute-start.10
  86.9 6.5 %y_part.4.unused.refs_1_ = bf16[256,256,128]{2,1,0:T(8,128)(2,1)} custom-call(bf16[256,256]{1,0:T(8,128)(2,1)S(1)} %after.20.wt_ref, bf16[2,256,256]{2,1,0:T(8,128)(2,1)S(1)} %g_pairs.1.g_ref.g, bf16[256,64,128]{2,1,0:T(8,128)(2,1)} %m_ref.1), custom_call_target="tpu_custom_call" | custom-call | flops 21474836480 | bytes 167772160 | tf_op jit(solution)/shard_map/y_part/pallas_call | solution.py:61
  95.3 6.5 %y_part.5.unused.refs_1_ = bf16[256,256,128]{2,1,0:T(8,128)(2,1)} custom-call(bf16[256,256]{1,0:T(8,128)(2,1)S(1)} %collective-permute-done.6.w, bf16[2,256,256]{2,1,0:T(8,128)(2,1)S(1)} %g_pairs.1.g_ref.g, bf16[256,64,128]{2,1,0:T(8,128)(2,1)} %after.17.m, bf16[256,256,128]{2,1,0:T(8,128)(2,1)} %y_part.4.unused.refs_1_), custom_call_target="tpu_custom_call", output_to_operand_aliasing={{}: (3, {})} | custom-call | flops 21474836480 | bytes 167772160 | tf_op jit(solution)/shard_map/y_part/pallas_call | solution.py:61
  105.8 3.1 %collective-permute-start.14 = (bf16[4,128,128]{2,1,0:T(8,128)(2,1)S(1)}, bf16[4,128,128]{2,1,0:T(8,128)(2,1)S(1)}, u32[]{:S(2)}, u32[]{:S(2)}) collective-permute-start(bf16[4,128,128]{2,1,0:T(8,128)(2,1)S(1)} %after.24), channel_id=1, source_target_pairs={{0,8},{4,12},{8,0},{12,4},{1,9},{5,13},{9,1},{13,5},{2,10},{6,14},... | collective-permute-start | bytes 393224 | tf_op jit(solution)/shard_map/ppermute | solution.py:17
  110.2 2.7 %collective-permute-start.19 = (bf16[4,128,128]{2,1,0:T(8,128)(2,1)S(1)}, bf16[4,128,128]{2,1,0:T(8,128)(2,1)S(1)}, u32[]{:S(2)}, u32[]{:S(2)}) collective-permute-start(bf16[4,128,128]{2,1,0:T(8,128)(2,1)S(1)} %collective-permute-done.17), channel_id=1, source_target_pairs={{0,112},{16,0},{32,16},{48,32},{64,48},{80,64},{96,80},{112,96},{1... | collective-permute-start | bytes 393224 | tf_op jit(solution)/shard_map/ppermute | solution.py:17
  115.5 5.0 %collective-permute-done.20 = bf16[4,128,128]{2,1,0:T(8,128)(2,1)S(1)} collective-permute-done((bf16[4,128,128]{2,1,0:T(8,128)(2,1)S(1)}, bf16[4,128,128]{2,1,0:T(8,128)(2,1)S(1)}, u32[]{:S(2)}, u32[]{:S(2)}) %collective-permute-start.20) | collective-permute-done | bytes 131104 | tf_op jit(solution)/shard_map/ppermute | solution.py:17
  120.6 2.7 %collective-permute-start.25 = (bf16[16,128,128]{2,1,0:T(8,128)(2,1)S(1)}, bf16[16,128,128]{2,1,0:T(8,128)(2,1)S(1)}, u32[]{:S(2)}, u32[]{:S(2)}) collective-permute-start(bf16[16,128,128]{2,1,0:T(8,128)(2,1)S(1)} %after.25.refs_7_), channel_id=1, source_target_pairs={{0,112},{16,0},{32,16},{48,32},{64,48},{80,64},{96,80},{112,96},{1... | collective-permute-start | bytes 1572872 | tf_op jit(solution)/shard_map/ppermute | solution.py:17
  123.3 6.5 %y_part.6.unused.refs_1_ = bf16[256,256,128]{2,1,0:T(8,128)(2,1)} custom-call(bf16[256,256]{1,0:T(8,128)(2,1)S(1)} %collective-permute-done.6.w, bf16[2,256,256]{2,1,0:T(8,128)(2,1)S(1)} %g_pairs.1.g_ref.g, bf16[256,64,128]{2,1,0:T(8,128)(2,1)} %after.19.m, bf16[256,256,128]{2,1,0:T(8,128)(2,1)} %y_part.5.unused.refs_1_), custom_call_target="tpu_custom_call", output_to_operand_aliasing={{}: (3, {})} | custom-call | flops 21474836480 | bytes 167772160 | tf_op jit(solution)/shard_map/y_part/pallas_call | solution.py:61
  129.9 2.5 %collective-permute-start.30 = (bf16[32,128,128]{2,1,0:T(8,128)(2,1)S(1)}, bf16[32,128,128]{2,1,0:T(8,128)(2,1)S(1)}, u32[]{:S(2)}, u32[]{:S(2)}) collective-permute-start(bf16[32,128,128]{2,1,0:T(8,128)(2,1)S(1)} %constant_dynamic-update-slice_fusion.refs_1_.refs_8_), channel_id=1, source_target_pairs={{0,12},{4,0},{8,4},{12,8},{1,13},{5,1},{9,5},{13,9},{2,14},{6,2},{... | collective-permute-start | bytes 3145736 | tf_op jit(solution)/shard_map/ppermute | solution.py:17
  133.9 6.5 %y_part.7.refs_1_.refs_2_.refs_3_.refs_4_.refs_5_.refs_6_.refs_7_.refs_8_.refs_9_.refs_10_.refs_11_.refs_12_.refs_13_.refs_14_.refs_15_.refs_16_.refs_17_.refs_18_.refs_19_.refs_20_.refs_21_.refs_22_.refs_23_.refs_24_ = bf16[256,256,128]{2,1,0:T(8,128)(2,1)} custom-call(bf16[256,256]{1,0:T(8,128)(2,1)S(1)} %get-tuple-element.12.w, ...), custom_call_target="tpu_custom_call", output_to_operand_aliasing={{}: (3, {})} | custom-call | flops 21474836480 | bytes 167772160 | tf_op jit(solution)/shard_map/y_part/pallas_call | solution.py:61
  141.3 3.5 %collective-permute-start.27 = (bf16[16,128,128]{2,1,0:T(8,128)(2,1)S(1)}, bf16[16,128,128]{2,1,0:T(8,128)(2,1)S(1)}, u32[]{:S(2)}, u32[]{:S(2)}) collective-permute-start(bf16[16,128,128]{2,1,0:T(8,128)(2,1)S(1)} %after.30.refs_28_), channel_id=1, source_target_pairs={{0,112},{16,0},{32,16},{48,32},{64,48},{80,64},{96,80},{112,96},{1... | collective-permute-start | bytes 1572872 | tf_op jit(solution)/shard_map/ppermute | solution.py:17
  144.8 4.8 %collective-permute-done.29.refs_31_ = bf16[32,128,128]{2,1,0:T(8,128)(2,1)S(1)} collective-permute-done((bf16[32,128,128]{2,1,0:T(8,128)(2,1)S(1)}, bf16[32,128,128]{2,1,0:T(8,128)(2,1)S(1)}, u32[]{:S(2)}, u32[]{:S(2)}) %collective-permute-start.29) | collective-permute-done | bytes 1048608 | tf_op jit(solution)/shard_map/ppermute | solution.py:17
  149.8 2.7 %collective-permute-start.32 = (bf16[16,128,128]{2,1,0:T(8,128)(2,1)S(1)}, bf16[16,128,128]{2,1,0:T(8,128)(2,1)S(1)}, u32[]{:S(2)}, u32[]{:S(2)}) collective-permute-start(bf16[16,128,128]{2,1,0:T(8,128)(2,1)S(1)} %slice.102), channel_id=1, source_target_pairs={{0,12},{4,0},{8,4},{12,8},{1,13},{5,1},{9,5},{13,9},{2,14},{6,2},{... | collective-permute-start | bytes 1572872 | tf_op jit(solution)/shard_map/ppermute | solution.py:17
  152.5 3.2 %contract.3.refs_1_.refs_35_ = f32[256,128]{1,0:T(8,128)S(1)} custom-call(s32[64]{0:T(128)S(1)} %fusion.7.refs_0_, bf16[256,256,128]{2,1,0:T(8,128)(2,1)} %y_part.7.refs_1_.refs_2_.refs_3_.refs_4_.refs_5_.refs_6_.refs_7_.refs_8_.refs_9_.refs_10_.refs_11_.refs_12_.refs_13_.refs_14_.refs_15_.refs_16_.refs_17_.refs_18_.refs_19_.refs_20_.refs_21_.refs_22_.refs_23_.refs_24_, ...), custom_call_target="tpu_custom_call" | custom-call | flops 402653184 | bytes 4718592 | tf_op jit(solution)/shard_map/contract/pallas_call | solution.py:132
  158.1 3.7 %collective-permute-done.31.refs_33_ = bf16[16,128,128]{2,1,0:T(8,128)(2,1)S(1)} collective-permute-done((bf16[16,128,128]{2,1,0:T(8,128)(2,1)S(1)}, bf16[16,128,128]{2,1,0:T(8,128)(2,1)S(1)}, u32[]{:S(2)}, u32[]{:S(2)}) %collective-permute-start.31) | collective-permute-done | bytes 524320 | tf_op jit(solution)/shard_map/ppermute | solution.py:17
  163.4 8.8 %contract.4.refs_5_ = f32[256,128]{1,0:T(8,128)S(1)} custom-call(s32[64]{0:T(128)S(1)} %fusion.7.refs_0_, bf16[256,256,128]{2,1,0:T(8,128)(2,1)} %y_part.7.refs_1_.refs_2_.refs_3_.refs_4_.refs_5_.refs_6_.refs_7_.refs_8_.refs_9_.refs_10_.refs_11_.refs_12_.refs_13_.refs_14_.refs_15_.refs_16_.refs_17_.refs_18_.refs_19_.refs_20_.refs_21_.refs_22_.refs_23_.refs_24_, ...), custom_call_target="tpu_custom_call" | custom-call | flops 1610612736 | bytes 18874368 | tf_op jit(solution)/shard_map/contract/pallas_call | solution.py:132
  172.3 2.3 %contract.5 = f32[256,128]{1,0:T(8,128)S(1)} custom-call(s32[64]{0:T(128)S(1)} %fusion.7.refs_0_, bf16[256,256,128]{2,1,0:T(8,128)(2,1)} %y_part.7.refs_1_.refs_2_.refs_3_.refs_4_.refs_5_.refs_6_.refs_7_.refs_8_.refs_9_.refs_10_.refs_11_.refs_12_.refs_13_.refs_14_.refs_15_.refs_16_.refs_17_.refs_18_.refs_19_.refs_20_.refs_21_.refs_22_.refs_23_.refs_24_, ...), custom_call_target="tpu_custom_call" | custom-call | flops 134217728 | bytes 1572864 | tf_op jit(solution)/shard_map/contract/pallas_call | solution.py:132
  175.4 15.6 %all-to-all-start.1 = ((f32[128,4,128]{2,1,0:T(4,128)}), f32[128,4,128]{2,1,0:T(4,128)S(1)}, u32[]{:S(2)}, u32[]{:S(2)}) async-start(f32[128,4,128]{2,1,0:T(4,128)} %bitcast.23), calls=%async_computation.1 | async-start | bytes 524288 | tf_op jit(solution)/shard_map/all_to_all | solution.py:395
  191.3 15.4 %all-to-all-done.1 = f32[128,4,128]{2,1,0:T(4,128)S(1)} async-done(((f32[128,4,128]{2,1,0:T(4,128)}), f32[128,4,128]{2,1,0:T(4,128)S(1)}, u32[]{:S(2)}, u32[]{:S(2)}) %all-to-all-start.1) | async-done | bytes 262176 | tf_op jit(solution)/shard_map/all_to_all | solution.py:395
  (164 shorter events, 43.6 us)
Async XLA Ops:
  1.0 12.9 %collective-permute-start.3 = (bf16[256,64,128]{2,1,0:T(8,128)(2,1)}, bf16[256,64,128]{2,1,0:T(8,128)(2,1)}, u32[]{:S(2)}, u32[]{:S(2)}) collective-permute-start(bf16[256,64,128]{2,1,0:T(8,128)(2,1)} %m_ref.1), channel_id=1, source_target_pairs={{0,2},{2,0},{1,3},{3,1},{4,6},{6,4},{5,7},{7,5},{8,10},{10,8},{9,1... | collective-permute-start | bytes 12582920 | tf_op jit(solution)/shard_map/ppermute | solution.py:17
  4.2 9.7 %collective-permute-start.2 = (bf16[256,512]{1,0:T(8,128)(2,1)}, bf16[256,512]{1,0:T(8,128)(2,1)S(1)}, u32[]{:S(2)}, u32[]{:S(2)}) collective-permute-start(bf16[256,512]{1,0:T(8,128)(2,1)} %bitcast.38), channel_id=1, source_target_pairs={{0,1},{1,0},{2,3},{3,2},{4,5},{5,4},{6,7},{7,6},{8,9},{9,8},{10,11... | collective-permute-start | bytes 786440 | tf_op jit(solution)/shard_map/ppermute | solution.py:17
  13.9 64.5 %collective-permute-start.4 = (bf16[256,64,128]{2,1,0:T(8,128)(2,1)}, bf16[256,64,128]{2,1,0:T(8,128)(2,1)}, u32[]{:S(2)}, u32[]{:S(2)}) collective-permute-start(bf16[256,64,128]{2,1,0:T(8,128)(2,1)} %after.17.m), channel_id=1, source_target_pairs={{0,128},{2,131},{128,1},{130,2},{1,129},{3,130},{129,0},{131,3},{4... | collective-permute-start | bytes 12582920 | tf_op jit(solution)/shard_map/ppermute | solution.py:284
  16.6 61.7 %all-to-all-start = ((bf16[128,64,128]{2,1,0:T(8,128)(2,1)}), bf16[128,64,128]{2,1,0:T(8,128)(2,1)S(1)}, u32[]{:S(2)}, u32[]{:S(2)}) async-start(bf16[128,64,128]{2,1,0:T(8,128)(2,1)} %after.18), calls=%async_computation | async-start | bytes 4194304 | tf_op jit(solution)/shard_map/all_to_all | solution.py:287
  81.9 13.4 %collective-permute-start.6 = (bf16[256,256]{1,0:T(8,128)(2,1)S(1)}, bf16[256,256]{1,0:T(8,128)(2,1)S(1)}, u32[]{:S(2)}, u32[]{:S(2)}) collective-permute-start(bf16[256,256]{1,0:T(8,128)(2,1)S(1)} %get-tuple-element.11), channel_id=1, source_target_pairs={{0,2},{2,0},{1,3},{3,1},{4,6},{6,4},{5,7},{7,5},{8,10},{10,8},{9,1... | collective-permute-start | bytes 393224 | tf_op jit(solution)/shard_map/ppermute | solution.py:17
  83.3 50.6 %collective-permute-start.5 = (bf16[256,64,128]{2,1,0:T(8,128)(2,1)}, bf16[256,64,128]{2,1,0:T(8,128)(2,1)}, u32[]{:S(2)}, u32[]{:S(2)}) collective-permute-start(bf16[256,64,128]{2,1,0:T(8,128)(2,1)} %after.19.m), channel_id=1, source_target_pairs={{0,2},{2,0},{1,3},{3,1},{4,6},{6,4},{5,7},{7,5},{8,10},{10,8},{9,1... | collective-permute-start | bytes 12582920 | tf_op jit(solution)/shard_map/ppermute | solution.py:17
  83.5 9.9 %collective-permute-start.8 = (bf16[4,64,128]{2,1,0:T(8,128)(2,1)S(1)}, bf16[4,64,128]{2,1,0:T(8,128)(2,1)S(1)}, u32[]{:S(2)}, u32[]{:S(2)}) collective-permute-start(bf16[4,64,128]{2,1,0:T(8,128)(2,1)S(1)} %get-tuple-element.10), channel_id=1, source_target_pairs={{0,1},{1,0},{2,3},{3,2},{4,5},{5,4},{6,7},{7,6},{8,9},{9,8},{10,11... | collective-permute-start | bytes 196616 | tf_op jit(solution)/shard_map/ppermute | solution.py:17
  84.4 9.0 %collective-permute-start.9 = (bf16[4,64,128]{2,1,0:T(8,128)(2,1)S(1)}, bf16[4,64,128]{2,1,0:T(8,128)(2,1)S(1)}, u32[]{:S(2)}, u32[]{:S(2)}) collective-permute-start(bf16[4,64,128]{2,1,0:T(8,128)(2,1)S(1)} %get-tuple-element.9), channel_id=1, source_target_pairs={{0,128},{128,0},{1,129},{129,1},{2,130},{130,2},{3,131},{131,3},{4... | collective-permute-start | bytes 196616 | tf_op jit(solution)/shard_map/ppermute | solution.py:17
  85.0 8.4 %collective-permute-start.10 = (bf16[4,64,128]{2,1,0:T(8,128)(2,1)S(1)}, bf16[4,64,128]{2,1,0:T(8,128)(2,1)S(1)}, u32[]{:S(2)}, u32[]{:S(2)}) collective-permute-start(bf16[4,64,128]{2,1,0:T(8,128)(2,1)S(1)} %get-tuple-element.8), channel_id=1, source_target_pairs={{0,129},{1,128},{128,1},{129,0},{2,131},{3,130},{130,3},{131,2},{4... | collective-permute-start | bytes 196616 | tf_op jit(solution)/shard_map/ppermute | solution.py:298
  93.7 9.8 %collective-permute-start.12 = (bf16[4,128,128]{2,1,0:T(8,128)(2,1)S(1)}, bf16[4,128,128]{2,1,0:T(8,128)(2,1)S(1)}, u32[]{:S(2)}, u32[]{:S(2)}) collective-permute-start(bf16[4,128,128]{2,1,0:T(8,128)(2,1)S(1)} %after.21), channel_id=1, source_target_pairs={{0,112},{16,0},{32,16},{48,32},{64,48},{80,64},{96,80},{112,96},{1... | collective-permute-start | bytes 393224 | tf_op jit(solution)/shard_map/ppermute | solution.py:17
  93.8 7.9 %collective-permute-start.11 = (bf16[4,128,128]{2,1,0:T(8,128)(2,1)S(1)}, bf16[4,128,128]{2,1,0:T(8,128)(2,1)S(1)}, u32[]{:S(2)}, u32[]{:S(2)}) collective-permute-start(bf16[4,128,128]{2,1,0:T(8,128)(2,1)S(1)} %after.21), channel_id=1, source_target_pairs={{0,16},{16,32},{32,48},{48,64},{64,80},{80,96},{96,112},{112,0},{1... | collective-permute-start | bytes 393224 | tf_op jit(solution)/shard_map/ppermute | solution.py:17
  120.5 12.0 %collective-permute-start.21 = (bf16[16,128,128]{2,1,0:T(8,128)(2,1)S(1)}, bf16[16,128,128]{2,1,0:T(8,128)(2,1)S(1)}, u32[]{:S(2)}, u32[]{:S(2)}) collective-permute-start(bf16[16,128,128]{2,1,0:T(8,128)(2,1)S(1)} %after.25.refs_7_), channel_id=1, source_target_pairs={{0,16},{16,32},{32,48},{48,64},{64,80},{80,96},{96,112},{112,0},{1... | collective-permute-start | bytes 1572872 | tf_op jit(solution)/shard_map/ppermute | solution.py:17
  120.6 11.8 %collective-permute-start.25 = (bf16[16,128,128]{2,1,0:T(8,128)(2,1)S(1)}, bf16[16,128,128]{2,1,0:T(8,128)(2,1)S(1)}, u32[]{:S(2)}, u32[]{:S(2)}) collective-permute-start(bf16[16,128,128]{2,1,0:T(8,128)(2,1)S(1)} %after.25.refs_7_), channel_id=1, source_target_pairs={{0,112},{16,0},{32,16},{48,32},{64,48},{80,64},{96,80},{112,96},{1... | collective-permute-start | bytes 1572872 | tf_op jit(solution)/shard_map/ppermute | solution.py:17
  129.8 19.8 %collective-permute-start.29 = (bf16[32,128,128]{2,1,0:T(8,128)(2,1)S(1)}, bf16[32,128,128]{2,1,0:T(8,128)(2,1)S(1)}, u32[]{:S(2)}, u32[]{:S(2)}) collective-permute-start(bf16[32,128,128]{2,1,0:T(8,128)(2,1)S(1)} %constant_dynamic-update-slice_fusion.refs_1_.refs_8_), channel_id=1, source_target_pairs={{0,4},{4,8},{8,12},{12,0},{1,5},{5,9},{9,13},{13,1},{2,6},{6,10},{... | collective-permute-start | bytes 3145736 | tf_op jit(solution)/shard_map/ppermute | solution.py:17
  129.9 19.8 %collective-permute-start.30 = (bf16[32,128,128]{2,1,0:T(8,128)(2,1)S(1)}, bf16[32,128,128]{2,1,0:T(8,128)(2,1)S(1)}, u32[]{:S(2)}, u32[]{:S(2)}) collective-permute-start(bf16[32,128,128]{2,1,0:T(8,128)(2,1)S(1)} %constant_dynamic-update-slice_fusion.refs_1_.refs_8_), channel_id=1, source_target_pairs={{0,12},{4,0},{8,4},{12,8},{1,13},{5,1},{9,5},{13,9},{2,14},{6,2},{... | collective-permute-start | bytes 3145736 | tf_op jit(solution)/shard_map/ppermute | solution.py:17
  132.5 8.8 %collective-permute-start.26 = (bf16[16,128,128]{2,1,0:T(8,128)(2,1)S(1)}, bf16[16,128,128]{2,1,0:T(8,128)(2,1)S(1)}, u32[]{:S(2)}, u32[]{:S(2)}) collective-permute-start(bf16[16,128,128]{2,1,0:T(8,128)(2,1)S(1)} %after.29.refs_26_), channel_id=1, source_target_pairs={{0,112},{16,0},{32,16},{48,32},{64,48},{80,64},{96,80},{112,96},{1... | collective-permute-start | bytes 1572872 | tf_op jit(solution)/shard_map/ppermute | solution.py:17
  132.5 12.2 %collective-permute-start.22 = (bf16[16,128,128]{2,1,0:T(8,128)(2,1)S(1)}, bf16[16,128,128]{2,1,0:T(8,128)(2,1)S(1)}, u32[]{:S(2)}, u32[]{:S(2)}) collective-permute-start(bf16[16,128,128]{2,1,0:T(8,128)(2,1)S(1)} %after.26.refs_25_), channel_id=1, source_target_pairs={{0,16},{16,32},{32,48},{48,64},{64,80},{80,96},{96,112},{112,0},{1... | collective-permute-start | bytes 1572872 | tf_op jit(solution)/shard_map/ppermute | solution.py:17
  141.3 14.5 %collective-permute-start.27 = (bf16[16,128,128]{2,1,0:T(8,128)(2,1)S(1)}, bf16[16,128,128]{2,1,0:T(8,128)(2,1)S(1)}, u32[]{:S(2)}, u32[]{:S(2)}) collective-permute-start(bf16[16,128,128]{2,1,0:T(8,128)(2,1)S(1)} %after.30.refs_28_), channel_id=1, source_target_pairs={{0,112},{16,0},{32,16},{48,32},{64,48},{80,64},{96,80},{112,96},{1... | collective-permute-start | bytes 1572872 | tf_op jit(solution)/shard_map/ppermute | solution.py:17
  144.8 13.1 %collective-permute-start.23 = (bf16[16,128,128]{2,1,0:T(8,128)(2,1)S(1)}, bf16[16,128,128]{2,1,0:T(8,128)(2,1)S(1)}, u32[]{:S(2)}, u32[]{:S(2)}) collective-permute-start(bf16[16,128,128]{2,1,0:T(8,128)(2,1)S(1)} %after.27.refs_27_), channel_id=1, source_target_pairs={{0,16},{16,32},{32,48},{48,64},{64,80},{80,96},{96,112},{112,0},{1... | collective-permute-start | bytes 1572872 | tf_op jit(solution)/shard_map/ppermute | solution.py:17
  149.6 12.2 %collective-permute-start.31 = (bf16[16,128,128]{2,1,0:T(8,128)(2,1)S(1)}, bf16[16,128,128]{2,1,0:T(8,128)(2,1)S(1)}, u32[]{:S(2)}, u32[]{:S(2)}) collective-permute-start(bf16[16,128,128]{2,1,0:T(8,128)(2,1)S(1)} %slice.101), channel_id=1, source_target_pairs={{0,4},{4,8},{8,12},{12,0},{1,5},{5,9},{9,13},{13,1},{2,6},{6,10},{... | collective-permute-start | bytes 1572872 | tf_op jit(solution)/shard_map/ppermute | solution.py:17
  149.8 12.0 %collective-permute-start.32 = (bf16[16,128,128]{2,1,0:T(8,128)(2,1)S(1)}, bf16[16,128,128]{2,1,0:T(8,128)(2,1)S(1)}, u32[]{:S(2)}, u32[]{:S(2)}) collective-permute-start(bf16[16,128,128]{2,1,0:T(8,128)(2,1)S(1)} %slice.102), channel_id=1, source_target_pairs={{0,12},{4,0},{8,4},{12,8},{1,13},{5,1},{9,5},{13,9},{2,14},{6,2},{... | collective-permute-start | bytes 1572872 | tf_op jit(solution)/shard_map/ppermute | solution.py:17
  155.9 16.4 %collective-permute-start.28 = (bf16[8,128,128]{2,1,0:T(8,128)(2,1)S(1)}, bf16[8,128,128]{2,1,0:T(8,128)(2,1)S(1)}, u32[]{:S(2)}, u32[]{:S(2)}) collective-permute-start(bf16[8,128,128]{2,1,0:T(8,128)(2,1)S(1)} %slice.100), channel_id=1, source_target_pairs={{0,112},{16,0},{32,16},{48,32},{64,48},{80,64},{96,80},{112,96},{1... | collective-permute-start | bytes 786440 | tf_op jit(solution)/shard_map/ppermute | solution.py:17
  157.9 14.4 %collective-permute-start.24 = (bf16[8,128,128]{2,1,0:T(8,128)(2,1)S(1)}, bf16[8,128,128]{2,1,0:T(8,128)(2,1)S(1)}, u32[]{:S(2)}, u32[]{:S(2)}) collective-permute-start(bf16[8,128,128]{2,1,0:T(8,128)(2,1)S(1)} %slice.99), channel_id=1, source_target_pairs={{0,16},{16,32},{32,48},{48,64},{64,80},{80,96},{96,112},{112,0},{1... | collective-permute-start | bytes 786440 | tf_op jit(solution)/shard_map/ppermute | solution.py:17
  175.4 31.3 %all-to-all-start.1 = ((f32[128,4,128]{2,1,0:T(4,128)}), f32[128,4,128]{2,1,0:T(4,128)S(1)}, u32[]{:S(2)}, u32[]{:S(2)}) async-start(f32[128,4,128]{2,1,0:T(4,128)} %bitcast.23), calls=%async_computation.1 | async-start | bytes 524288 | tf_op jit(solution)/shard_map/all_to_all | solution.py:395
  (29 other events, 201.0 us)

commit v2 on v1

--- a/solution.py
+++ b/solution.py
@@ -7,7 +7,7 @@
 
 NZ, NX, NC = 8, 4, 2
 CHIPS = NZ * NX
-VMEM = 52 << 20
+VMEM = 49 << 20
 BF = jnp.bfloat16
 F32 = jnp.float32
 

time: 208 us -> 205 us (0.986)
  Pallas kernels: 46.1 us -> 40.2 us
  starting transfers between devices: 67.4 us -> 70.9 us
    all_to_all x1, starting transfers between devices: 15.6 us -> 18.8 us  [body(): moved = lax.all_to_all(partial, ('z', 'x', 'core', 'ao'), 0, 0, tiled=True)]
    pallas_call x4, Pallas kernels: 26 us -> 23 us  [y_part(): pl.pallas_call(kernel, grid=(steps,), in_specs=specs, out_specs=pl.BlockS...]
    unnamed x46 -> x38, local copies, waits for them, and re-layouts: 5.29 us -> 3.91 us
  transfers between devices with their start and end apart: 35 -> 35, of which waited for: 11 -> 12; matrix products, arithmetic and copies ran while one was open for 7% -> 7% of each run, Pallas kernels for 20% -> 18%
where the time goes in v2:
time: 205 us
  waiting for transfers between devices  74.6 us (36%)
  starting transfers between devices  70.9 us (35%)
  Pallas kernels  40.2 us (20%)
  other arithmetic  10.7 us (5%)
  local copies, waits for them, and re-layouts  7.29 us (4%)
    all_to_all x1, waiting for transfers between devices, body(): lax.all_to_all(send, ('z', 'x'), 0, 0, tiled=True)  36.5 us
    ppermute x29, starting transfers between devices, shift(): return lax.ppermute(value, axis, [(i, (i + by) % n) for i in range(n)])  36.1 us
    pallas_call x4, Pallas kernels, y_part(): pl.pallas_call(kernel, grid=(steps,), in_specs=specs, out_specs=pl.BlockS...  23 us
    ppermute x29, waiting for transfers between devices, shift(): return lax.ppermute(value, axis, [(i, (i + by) % n) for i in range(n)])  22 us
    all_to_all x1, starting transfers between devices, body(): moved = lax.all_to_all(partial, ('z', 'x', 'core', 'ao'), 0, 0, tiled=True)  18.8 us
    all_to_all x1, waiting for transfers between devices, body(): moved = lax.all_to_all(partial, ('z', 'x', 'core', 'ao'), 0, 0, tiled=True)  15.4 us
    pallas_call x3, Pallas kernels, contract(): pl.pallas_call(lambda *refs: contract_kernel(counts, before is not None,...  13.6 us
    all_to_all x1, starting transfers between devices, body(): lax.all_to_all(send, ('z', 'x'), 0, 0, tiled=True)  13.1 us
  transfers between devices with their start and end apart: 35, of which 12 were waited for; matrix products, arithmetic and copies ran while one was open for 7% of the time, Pallas kernels for 18%

profile of v2, /device:TPU:1, one launch (start us, length us, event | category | flops | bytes accessed | tf_op | source)
XLA Modules:
  0.0 204.7 jit_solution(12156074707786275543)
XLA Ops:
  1.0 3.2 %collective-permute-start.3 = (bf16[256,64,128]{2,1,0:T(8,128)(2,1)}, bf16[256,64,128]{2,1,0:T(8,128)(2,1)}, u32[]{:S(2)}, u32[]{:S(2)}) collective-permute-start(bf16[256,64,128]{2,1,0:T(8,128)(2,1)} %m_ref.1), channel_id=1, source_target_pairs={{0,2},{2,0},{1,3},{3,1},{4,6},{6,4},{5,7},{7,5},{8,10},{10,8},{9,1... | collective-permute-start | bytes 12582920 | tf_op jit(solution)/shard_map/ppermute | solution.py:17
  9.9 4.0 %collective-permute-done.2.oth_ref.refs_1_ = bf16[256,512]{1,0:T(8,128)(2,1)S(1)} collective-permute-done((bf16[256,512]{1,0:T(8,128)(2,1)}, bf16[256,512]{1,0:T(8,128)(2,1)S(1)}, u32[]{:S(2)}, u32[]{:S(2)}) %collective-permute-start.2) | collective-permute-done | bytes 262176 | tf_op jit(solution)/shard_map/ppermute | solution.py:17
  17.0 13.1 %all-to-all-start = ((bf16[128,64,128]{2,1,0:T(8,128)(2,1)}), bf16[128,64,128]{2,1,0:T(8,128)(2,1)S(1)}, u32[]{:S(2)}, u32[]{:S(2)}) async-start(bf16[128,64,128]{2,1,0:T(8,128)(2,1)} %copy-done), calls=%async_computation | async-start | bytes 4194304 | tf_op jit(solution)/shard_map/all_to_all | solution.py:287
  42.1 36.5 %all-to-all-done = bf16[128,64,128]{2,1,0:T(8,128)(2,1)S(1)} async-done(((bf16[128,64,128]{2,1,0:T(8,128)(2,1)}), bf16[128,64,128]{2,1,0:T(8,128)(2,1)S(1)}, u32[]{:S(2)}, u32[]{:S(2)}) %all-to-all-start) | async-done | bytes 2097184 | tf_op jit(solution)/shard_map/all_to_all | solution.py:287
  81.8 3.6 %collective-permute-start.8 = (bf16[4,64,128]{2,1,0:T(8,128)(2,1)S(1)}, bf16[4,64,128]{2,1,0:T(8,128)(2,1)S(1)}, u32[]{:S(2)}, u32[]{:S(2)}) collective-permute-start(bf16[4,64,128]{2,1,0:T(8,128)(2,1)S(1)} %get-tuple-element.10), channel_id=1, source_target_pairs={{0,1},{1,0},{2,3},{3,2},{4,5},{5,4},{6,7},{7,6},{8,9},{9,8},{10,11... | collective-permute-start | bytes 196616 | tf_op jit(solution)/shard_map/ppermute | solution.py:17
  85.7 5.0 %y_part.4.unused.refs_1_ = bf16[256,256,128]{2,1,0:T(8,128)(2,1)} custom-call(bf16[256,256]{1,0:T(8,128)(2,1)S(1)} %after.20.wt_ref, bf16[2,256,256]{2,1,0:T(8,128)(2,1)S(1)} %g_pairs.1.g_ref.g, bf16[256,64,128]{2,1,0:T(8,128)(2,1)S(1)} %copy-done.1), custom_call_target="tpu_custom_call" | custom-call | flops 21474836480 | bytes 167772160 | tf_op jit(solution)/shard_map/y_part/pallas_call | solution.py:61
  92.6 6.5 %y_part.5.unused.refs_1_ = bf16[256,256,128]{2,1,0:T(8,128)(2,1)} custom-call(bf16[256,256]{1,0:T(8,128)(2,1)S(1)} %collective-permute-done.6.w, bf16[2,256,256]{2,1,0:T(8,128)(2,1)S(1)} %g_pairs.1.g_ref.g, bf16[256,64,128]{2,1,0:T(8,128)(2,1)} %after.17.m, bf16[256,256,128]{2,1,0:T(8,128)(2,1)} %y_part.4.unused.refs_1_), custom_call_target="tpu_custom_call", output_to_operand_aliasing={{}: (3, {})} | custom-call | flops 21474836480 | bytes 167772160 | tf_op jit(solution)/shard_map/y_part/pallas_call | solution.py:61
  103.0 2.3 %collective-permute-start.14 = (bf16[4,128,128]{2,1,0:T(8,128)(2,1)S(1)}, bf16[4,128,128]{2,1,0:T(8,128)(2,1)S(1)}, u32[]{:S(2)}, u32[]{:S(2)}) collective-permute-start(bf16[4,128,128]{2,1,0:T(8,128)(2,1)S(1)} %after.24), channel_id=1, source_target_pairs={{0,8},{4,12},{8,0},{12,4},{1,9},{5,13},{9,1},{13,5},{2,10},{6,14},... | collective-permute-start | bytes 393224 | tf_op jit(solution)/shard_map/ppermute | solution.py:17
  106.9 2.4 %collective-permute-start.19 = (bf16[4,128,128]{2,1,0:T(8,128)(2,1)S(1)}, bf16[4,128,128]{2,1,0:T(8,128)(2,1)S(1)}, u32[]{:S(2)}, u32[]{:S(2)}) collective-permute-start(bf16[4,128,128]{2,1,0:T(8,128)(2,1)S(1)} %collective-permute-done.17), channel_id=1, source_target_pairs={{0,112},{16,0},{32,16},{48,32},{64,48},{80,64},{96,80},{112,96},{1... | collective-permute-start | bytes 393224 | tf_op jit(solution)/shard_map/ppermute | solution.py:17
  112.0 5.0 %collective-permute-done.20 = bf16[4,128,128]{2,1,0:T(8,128)(2,1)S(1)} collective-permute-done((bf16[4,128,128]{2,1,0:T(8,128)(2,1)S(1)}, bf16[4,128,128]{2,1,0:T(8,128)(2,1)S(1)}, u32[]{:S(2)}, u32[]{:S(2)}) %collective-permute-start.20) | collective-permute-done | bytes 131104 | tf_op jit(solution)/shard_map/ppermute | solution.py:17
  117.1 2.7 %collective-permute-start.25 = (bf16[16,128,128]{2,1,0:T(8,128)(2,1)S(1)}, bf16[16,128,128]{2,1,0:T(8,128)(2,1)S(1)}, u32[]{:S(2)}, u32[]{:S(2)}) collective-permute-start(bf16[16,128,128]{2,1,0:T(8,128)(2,1)S(1)} %after.25.refs_7_), channel_id=1, source_target_pairs={{0,112},{16,0},{32,16},{48,32},{64,48},{80,64},{96,80},{112,96},{1... | collective-permute-start | bytes 1572872 | tf_op jit(solution)/shard_map/ppermute | solution.py:17
  119.7 6.5 %y_part.6.unused.refs_1_ = bf16[256,256,128]{2,1,0:T(8,128)(2,1)} custom-call(bf16[256,256]{1,0:T(8,128)(2,1)S(1)} %collective-permute-done.6.w, bf16[2,256,256]{2,1,0:T(8,128)(2,1)S(1)} %g_pairs.1.g_ref.g, bf16[256,64,128]{2,1,0:T(8,128)(2,1)} %after.19.m, bf16[256,256,128]{2,1,0:T(8,128)(2,1)} %y_part.5.unused.refs_1_), custom_call_target="tpu_custom_call", output_to_operand_aliasing={{}: (3, {})} | custom-call | flops 21474836480 | bytes 167772160 | tf_op jit(solution)/shard_map/y_part/pallas_call | solution.py:61
  126.4 2.5 %collective-permute-start.30 = (bf16[32,128,128]{2,1,0:T(8,128)(2,1)S(1)}, bf16[32,128,128]{2,1,0:T(8,128)(2,1)S(1)}, u32[]{:S(2)}, u32[]{:S(2)}) collective-permute-start(bf16[32,128,128]{2,1,0:T(8,128)(2,1)S(1)} %constant_dynamic-update-slice_fusion.refs_1_.refs_8_), channel_id=1, source_target_pairs={{0,12},{4,0},{8,4},{12,8},{1,13},{5,1},{9,5},{13,9},{2,14},{6,2},{... | collective-permute-start | bytes 3145736 | tf_op jit(solution)/shard_map/ppermute | solution.py:17
  130.4 5.0 %y_part.7.refs_1_.refs_2_.refs_3_.refs_4_.refs_5_.refs_6_.refs_7_.refs_8_.refs_9_.refs_10_.refs_11_.refs_12_.refs_13_.refs_14_.refs_15_.refs_16_.refs_17_.refs_18_.refs_19_.refs_20_.refs_21_.refs_22_.refs_23_.refs_24_ = bf16[256,256,128]{2,1,0:T(8,128)(2,1)} custom-call(bf16[256,256]{1,0:T(8,128)(2,1)S(1)} %get-tuple-element.12.w, ...), custom_call_target="tpu_custom_call", output_to_operand_aliasing={{}: (3, {})} | custom-call | flops 21474836480 | bytes 167772160 | tf_op jit(solution)/shard_map/y_part/pallas_call | solution.py:61
  135.4 2.6 %collective-permute-done.26.refs_0_ = bf16[16,128,128]{2,1,0:T(8,128)(2,1)S(1)} collective-permute-done((bf16[16,128,128]{2,1,0:T(8,128)(2,1)S(1)}, bf16[16,128,128]{2,1,0:T(8,128)(2,1)S(1)}, u32[]{:S(2)}, u32[]{:S(2)}) %collective-permute-start.26) | collective-permute-done | bytes 524320 | tf_op jit(solution)/shard_map/ppermute | solution.py:17
  138.0 3.5 %collective-permute-start.27 = (bf16[16,128,128]{2,1,0:T(8,128)(2,1)S(1)}, bf16[16,128,128]{2,1,0:T(8,128)(2,1)S(1)}, u32[]{:S(2)}, u32[]{:S(2)}) collective-permute-start(bf16[16,128,128]{2,1,0:T(8,128)(2,1)S(1)} %after.30.refs_28_), channel_id=1, source_target_pairs={{0,112},{16,0},{32,16},{48,32},{64,48},{80,64},{96,80},{112,96},{1... | collective-permute-start | bytes 1572872 | tf_op jit(solution)/shard_map/ppermute | solution.py:17
  141.5 4.3 %collective-permute-done.29.refs_31_ = bf16[32,128,128]{2,1,0:T(8,128)(2,1)S(1)} collective-permute-done((bf16[32,128,128]{2,1,0:T(8,128)(2,1)S(1)}, bf16[32,128,128]{2,1,0:T(8,128)(2,1)S(1)}, u32[]{:S(2)}, u32[]{:S(2)}) %collective-permute-start.29) | collective-permute-done | bytes 1048608 | tf_op jit(solution)/shard_map/ppermute | solution.py:17
  146.0 2.7 %collective-permute-start.32 = (bf16[16,128,128]{2,1,0:T(8,128)(2,1)S(1)}, bf16[16,128,128]{2,1,0:T(8,128)(2,1)S(1)}, u32[]{:S(2)}, u32[]{:S(2)}) collective-permute-start(bf16[16,128,128]{2,1,0:T(8,128)(2,1)S(1)} %slice.102), channel_id=1, source_target_pairs={{0,12},{4,0},{8,4},{12,8},{1,13},{5,1},{9,5},{13,9},{2,14},{6,2},{... | collective-permute-start | bytes 1572872 | tf_op jit(solution)/shard_map/ppermute | solution.py:17
  148.7 3.2 %contract.3.refs_1_.refs_35_ = f32[256,128]{1,0:T(8,128)S(1)} custom-call(s32[64]{0:T(128)S(1)} %fusion.7.refs_0_, bf16[256,256,128]{2,1,0:T(8,128)(2,1)} %y_part.7.refs_1_.refs_2_.refs_3_.refs_4_.refs_5_.refs_6_.refs_7_.refs_8_.refs_9_.refs_10_.refs_11_.refs_12_.refs_13_.refs_14_.refs_15_.refs_16_.refs_17_.refs_18_.refs_19_.refs_20_.refs_21_.refs_22_.refs_23_.refs_24_, ...), custom_call_target="tpu_custom_call" | custom-call | flops 402653184 | bytes 4718592 | tf_op jit(solution)/shard_map/contract/pallas_call | solution.py:132
  152.1 2.7 %collective-permute-start.28 = (bf16[8,128,128]{2,1,0:T(8,128)(2,1)S(1)}, bf16[8,128,128]{2,1,0:T(8,128)(2,1)S(1)}, u32[]{:S(2)}, u32[]{:S(2)}) collective-permute-start(bf16[8,128,128]{2,1,0:T(8,128)(2,1)S(1)} %slice.100), channel_id=1, source_target_pairs={{0,112},{16,0},{32,16},{48,32},{64,48},{80,64},{96,80},{112,96},{1... | collective-permute-start | bytes 786440 | tf_op jit(solution)/shard_map/ppermute | solution.py:17
  155.1 3.1 %collective-permute-done.31.refs_33_ = bf16[16,128,128]{2,1,0:T(8,128)(2,1)S(1)} collective-permute-done((bf16[16,128,128]{2,1,0:T(8,128)(2,1)S(1)}, bf16[16,128,128]{2,1,0:T(8,128)(2,1)S(1)}, u32[]{:S(2)}, u32[]{:S(2)}) %collective-permute-start.31) | collective-permute-done | bytes 524320 | tf_op jit(solution)/shard_map/ppermute | solution.py:17
  158.3 8.1 %contract.4.refs_5_ = f32[256,128]{1,0:T(8,128)S(1)} custom-call(s32[64]{0:T(128)S(1)} %fusion.7.refs_0_, bf16[256,256,128]{2,1,0:T(8,128)(2,1)} %y_part.7.refs_1_.refs_2_.refs_3_.refs_4_.refs_5_.refs_6_.refs_7_.refs_8_.refs_9_.refs_10_.refs_11_.refs_12_.refs_13_.refs_14_.refs_15_.refs_16_.refs_17_.refs_18_.refs_19_.refs_20_.refs_21_.refs_22_.refs_23_.refs_24_, ...), custom_call_target="tpu_custom_call" | custom-call | flops 1610612736 | bytes 18874368 | tf_op jit(solution)/shard_map/contract/pallas_call | solution.py:132
  169.5 18.8 %all-to-all-start.1 = ((f32[128,4,128]{2,1,0:T(4,128)}), f32[128,4,128]{2,1,0:T(4,128)S(1)}, u32[]{:S(2)}, u32[]{:S(2)}) async-start(f32[128,4,128]{2,1,0:T(4,128)} %bitcast.23), calls=%async_computation.1 | async-start | bytes 524288 | tf_op jit(solution)/shard_map/all_to_all | solution.py:395
  188.5 15.4 %all-to-all-done.1 = f32[128,4,128]{2,1,0:T(4,128)S(1)} async-done(((f32[128,4,128]{2,1,0:T(4,128)}), f32[128,4,128]{2,1,0:T(4,128)S(1)}, u32[]{:S(2)}, u32[]{:S(2)}) %all-to-all-start.1) | async-done | bytes 262176 | tf_op jit(solution)/shard_map/all_to_all | solution.py:395
  (156 shorter events, 41.5 us)
Async XLA Ops:
  1.0 12.9 %collective-permute-start.3 = (bf16[256,64,128]{2,1,0:T(8,128)(2,1)}, bf16[256,64,128]{2,1,0:T(8,128)(2,1)}, u32[]{:S(2)}, u32[]{:S(2)}) collective-permute-start(bf16[256,64,128]{2,1,0:T(8,128)(2,1)} %m_ref.1), channel_id=1, source_target_pairs={{0,2},{2,0},{1,3},{3,1},{4,6},{6,4},{5,7},{7,5},{8,10},{10,8},{9,1... | collective-permute-start | bytes 12582920 | tf_op jit(solution)/shard_map/ppermute | solution.py:17
  4.2 9.7 %collective-permute-start.2 = (bf16[256,512]{1,0:T(8,128)(2,1)}, bf16[256,512]{1,0:T(8,128)(2,1)S(1)}, u32[]{:S(2)}, u32[]{:S(2)}) collective-permute-start(bf16[256,512]{1,0:T(8,128)(2,1)} %bitcast.46), channel_id=1, source_target_pairs={{0,1},{1,0},{2,3},{3,2},{4,5},{5,4},{6,7},{7,6},{8,9},{9,8},{10,11... | collective-permute-start | bytes 786440 | tf_op jit(solution)/shard_map/ppermute | solution.py:17
  8.4 6.5 %collective-permute-start = (bf16[256,512]{1,0:T(8,128)(2,1)S(1)}, bf16[256,512]{1,0:T(8,128)(2,1)S(1)}, u32[]{:S(2)}, u32[]{:S(2)}) collective-permute-start(bf16[256,512]{1,0:T(8,128)(2,1)S(1)} %after.16), channel_id=1, source_target_pairs={{0,2},{2,4},{4,6},{6,8},{8,10},{10,12},{12,14},{14,16},{16,18},{18... | collective-permute-start | bytes 786440 | tf_op jit(solution)/shard_map/ppermute | solution.py:266
  13.9 64.8 %collective-permute-start.4 = (bf16[256,64,128]{2,1,0:T(8,128)(2,1)}, bf16[256,64,128]{2,1,0:T(8,128)(2,1)}, u32[]{:S(2)}, u32[]{:S(2)}) collective-permute-start(bf16[256,64,128]{2,1,0:T(8,128)(2,1)} %after.17.m), channel_id=1, source_target_pairs={{0,128},{2,131},{128,1},{130,2},{1,129},{3,130},{129,0},{131,3},{4... | collective-permute-start | bytes 12582920 | tf_op jit(solution)/shard_map/ppermute | solution.py:284
  17.0 61.7 %all-to-all-start = ((bf16[128,64,128]{2,1,0:T(8,128)(2,1)}), bf16[128,64,128]{2,1,0:T(8,128)(2,1)S(1)}, u32[]{:S(2)}, u32[]{:S(2)}) async-start(bf16[128,64,128]{2,1,0:T(8,128)(2,1)} %copy-done), calls=%async_computation | async-start | bytes 4194304 | tf_op jit(solution)/shard_map/all_to_all | solution.py:287
  80.2 12.4 %collective-permute-start.6 = (bf16[256,256]{1,0:T(8,128)(2,1)S(1)}, bf16[256,256]{1,0:T(8,128)(2,1)S(1)}, u32[]{:S(2)}, u32[]{:S(2)}) collective-permute-start(bf16[256,256]{1,0:T(8,128)(2,1)S(1)} %get-tuple-element.11), channel_id=1, source_target_pairs={{0,2},{2,0},{1,3},{3,1},{4,6},{6,4},{5,7},{7,5},{8,10},{10,8},{9,1... | collective-permute-start | bytes 393224 | tf_op jit(solution)/shard_map/ppermute | solution.py:17
  81.3 49.1 %collective-permute-start.5 = (bf16[256,64,128]{2,1,0:T(8,128)(2,1)}, bf16[256,64,128]{2,1,0:T(8,128)(2,1)S(1)}, u32[]{:S(2)}, u32[]{:S(2)}) collective-permute-start(bf16[256,64,128]{2,1,0:T(8,128)(2,1)} %after.19.m), channel_id=1, source_target_pairs={{0,2},{2,0},{1,3},{3,1},{4,6},{6,4},{5,7},{7,5},{8,10},{10,8},{9,1... | collective-permute-start | bytes 12582920 | tf_op jit(solution)/shard_map/ppermute | solution.py:17
  81.8 9.0 %collective-permute-start.8 = (bf16[4,64,128]{2,1,0:T(8,128)(2,1)S(1)}, bf16[4,64,128]{2,1,0:T(8,128)(2,1)S(1)}, u32[]{:S(2)}, u32[]{:S(2)}) collective-permute-start(bf16[4,64,128]{2,1,0:T(8,128)(2,1)S(1)} %get-tuple-element.10), channel_id=1, source_target_pairs={{0,1},{1,0},{2,3},{3,2},{4,5},{5,4},{6,7},{7,6},{8,9},{9,8},{10,11... | collective-permute-start | bytes 196616 | tf_op jit(solution)/shard_map/ppermute | solution.py:17
  91.0 9.2 %collective-permute-start.12 = (bf16[4,128,128]{2,1,0:T(8,128)(2,1)S(1)}, bf16[4,128,128]{2,1,0:T(8,128)(2,1)S(1)}, u32[]{:S(2)}, u32[]{:S(2)}) collective-permute-start(bf16[4,128,128]{2,1,0:T(8,128)(2,1)S(1)} %after.21), channel_id=1, source_target_pairs={{0,112},{16,0},{32,16},{48,32},{64,48},{80,64},{96,80},{112,96},{1... | collective-permute-start | bytes 393224 | tf_op jit(solution)/shard_map/ppermute | solution.py:17
  91.1 7.9 %collective-permute-start.11 = (bf16[4,128,128]{2,1,0:T(8,128)(2,1)S(1)}, bf16[4,128,128]{2,1,0:T(8,128)(2,1)S(1)}, u32[]{:S(2)}, u32[]{:S(2)}) collective-permute-start(bf16[4,128,128]{2,1,0:T(8,128)(2,1)S(1)} %after.21), channel_id=1, source_target_pairs={{0,16},{16,32},{32,48},{48,64},{64,80},{80,96},{96,112},{112,0},{1... | collective-permute-start | bytes 393224 | tf_op jit(solution)/shard_map/ppermute | solution.py:17
  103.0 6.3 %collective-permute-start.14 = (bf16[4,128,128]{2,1,0:T(8,128)(2,1)S(1)}, bf16[4,128,128]{2,1,0:T(8,128)(2,1)S(1)}, u32[]{:S(2)}, u32[]{:S(2)}) collective-permute-start(bf16[4,128,128]{2,1,0:T(8,128)(2,1)S(1)} %after.24), channel_id=1, source_target_pairs={{0,8},{4,12},{8,0},{12,4},{1,9},{5,13},{9,1},{13,5},{2,10},{6,14},... | collective-permute-start | bytes 393224 | tf_op jit(solution)/shard_map/ppermute | solution.py:17
  117.0 12.0 %collective-permute-start.21 = (bf16[16,128,128]{2,1,0:T(8,128)(2,1)S(1)}, bf16[16,128,128]{2,1,0:T(8,128)(2,1)S(1)}, u32[]{:S(2)}, u32[]{:S(2)}) collective-permute-start(bf16[16,128,128]{2,1,0:T(8,128)(2,1)S(1)} %after.25.refs_7_), channel_id=1, source_target_pairs={{0,16},{16,32},{32,48},{48,64},{64,80},{80,96},{96,112},{112,0},{1... | collective-permute-start | bytes 1572872 | tf_op jit(solution)/shard_map/ppermute | solution.py:17
  117.1 11.8 %collective-permute-start.25 = (bf16[16,128,128]{2,1,0:T(8,128)(2,1)S(1)}, bf16[16,128,128]{2,1,0:T(8,128)(2,1)S(1)}, u32[]{:S(2)}, u32[]{:S(2)}) collective-permute-start(bf16[16,128,128]{2,1,0:T(8,128)(2,1)S(1)} %after.25.refs_7_), channel_id=1, source_target_pairs={{0,112},{16,0},{32,16},{48,32},{64,48},{80,64},{96,80},{112,96},{1... | collective-permute-start | bytes 1572872 | tf_op jit(solution)/shard_map/ppermute | solution.py:17
  126.2 19.5 %collective-permute-start.29 = (bf16[32,128,128]{2,1,0:T(8,128)(2,1)S(1)}, bf16[32,128,128]{2,1,0:T(8,128)(2,1)S(1)}, u32[]{:S(2)}, u32[]{:S(2)}) collective-permute-start(bf16[32,128,128]{2,1,0:T(8,128)(2,1)S(1)} %constant_dynamic-update-slice_fusion.refs_1_.refs_8_), channel_id=1, source_target_pairs={{0,4},{4,8},{8,12},{12,0},{1,5},{5,9},{9,13},{13,1},{2,6},{6,10},{... | collective-permute-start | bytes 3145736 | tf_op jit(solution)/shard_map/ppermute | solution.py:17
  126.4 19.5 %collective-permute-start.30 = (bf16[32,128,128]{2,1,0:T(8,128)(2,1)S(1)}, bf16[32,128,128]{2,1,0:T(8,128)(2,1)S(1)}, u32[]{:S(2)}, u32[]{:S(2)}) collective-permute-start(bf16[32,128,128]{2,1,0:T(8,128)(2,1)S(1)} %constant_dynamic-update-slice_fusion.refs_1_.refs_8_), channel_id=1, source_target_pairs={{0,12},{4,0},{8,4},{12,8},{1,13},{5,1},{9,5},{13,9},{2,14},{6,2},{... | collective-permute-start | bytes 3145736 | tf_op jit(solution)/shard_map/ppermute | solution.py:17
  128.9 9.1 %collective-permute-start.26 = (bf16[16,128,128]{2,1,0:T(8,128)(2,1)S(1)}, bf16[16,128,128]{2,1,0:T(8,128)(2,1)S(1)}, u32[]{:S(2)}, u32[]{:S(2)}) collective-permute-start(bf16[16,128,128]{2,1,0:T(8,128)(2,1)S(1)} %after.29.refs_26_), channel_id=1, source_target_pairs={{0,112},{16,0},{32,16},{48,32},{64,48},{80,64},{96,80},{112,96},{1... | collective-permute-start | bytes 1572872 | tf_op jit(solution)/shard_map/ppermute | solution.py:17
  129.0 12.5 %collective-permute-start.22 = (bf16[16,128,128]{2,1,0:T(8,128)(2,1)S(1)}, bf16[16,128,128]{2,1,0:T(8,128)(2,1)S(1)}, u32[]{:S(2)}, u32[]{:S(2)}) collective-permute-start(bf16[16,128,128]{2,1,0:T(8,128)(2,1)S(1)} %after.26.refs_25_), channel_id=1, source_target_pairs={{0,16},{16,32},{32,48},{48,64},{64,80},{80,96},{96,112},{112,0},{1... | collective-permute-start | bytes 1572872 | tf_op jit(solution)/shard_map/ppermute | solution.py:17
  138.0 14.0 %collective-permute-start.27 = (bf16[16,128,128]{2,1,0:T(8,128)(2,1)S(1)}, bf16[16,128,128]{2,1,0:T(8,128)(2,1)S(1)}, u32[]{:S(2)}, u32[]{:S(2)}) collective-permute-start(bf16[16,128,128]{2,1,0:T(8,128)(2,1)S(1)} %after.30.refs_28_), channel_id=1, source_target_pairs={{0,112},{16,0},{32,16},{48,32},{64,48},{80,64},{96,80},{112,96},{1... | collective-permute-start | bytes 1572872 | tf_op jit(solution)/shard_map/ppermute | solution.py:17
  141.5 13.4 %collective-permute-start.23 = (bf16[16,128,128]{2,1,0:T(8,128)(2,1)S(1)}, bf16[16,128,128]{2,1,0:T(8,128)(2,1)S(1)}, u32[]{:S(2)}, u32[]{:S(2)}) collective-permute-start(bf16[16,128,128]{2,1,0:T(8,128)(2,1)S(1)} %after.27.refs_27_), channel_id=1, source_target_pairs={{0,16},{16,32},{32,48},{48,64},{64,80},{80,96},{96,112},{112,0},{1... | collective-permute-start | bytes 1572872 | tf_op jit(solution)/shard_map/ppermute | solution.py:17
  145.8 12.4 %collective-permute-start.31 = (bf16[16,128,128]{2,1,0:T(8,128)(2,1)S(1)}, bf16[16,128,128]{2,1,0:T(8,128)(2,1)S(1)}, u32[]{:S(2)}, u32[]{:S(2)}) collective-permute-start(bf16[16,128,128]{2,1,0:T(8,128)(2,1)S(1)} %slice.101), channel_id=1, source_target_pairs={{0,4},{4,8},{8,12},{12,0},{1,5},{5,9},{9,13},{13,1},{2,6},{6,10},{... | collective-permute-start | bytes 1572872 | tf_op jit(solution)/shard_map/ppermute | solution.py:17
  146.0 12.3 %collective-permute-start.32 = (bf16[16,128,128]{2,1,0:T(8,128)(2,1)S(1)}, bf16[16,128,128]{2,1,0:T(8,128)(2,1)S(1)}, u32[]{:S(2)}, u32[]{:S(2)}) collective-permute-start(bf16[16,128,128]{2,1,0:T(8,128)(2,1)S(1)} %slice.102), channel_id=1, source_target_pairs={{0,12},{4,0},{8,4},{12,8},{1,13},{5,1},{9,5},{13,9},{2,14},{6,2},{... | collective-permute-start | bytes 1572872 | tf_op jit(solution)/shard_map/ppermute | solution.py:17
  152.1 14.3 %collective-permute-start.28 = (bf16[8,128,128]{2,1,0:T(8,128)(2,1)S(1)}, bf16[8,128,128]{2,1,0:T(8,128)(2,1)S(1)}, u32[]{:S(2)}, u32[]{:S(2)}) collective-permute-start(bf16[8,128,128]{2,1,0:T(8,128)(2,1)S(1)} %slice.100), channel_id=1, source_target_pairs={{0,112},{16,0},{32,16},{48,32},{64,48},{80,64},{96,80},{112,96},{1... | collective-permute-start | bytes 786440 | tf_op jit(solution)/shard_map/ppermute | solution.py:17
  154.9 11.5 %collective-permute-start.24 = (bf16[8,128,128]{2,1,0:T(8,128)(2,1)S(1)}, bf16[8,128,128]{2,1,0:T(8,128)(2,1)S(1)}, u32[]{:S(2)}, u32[]{:S(2)}) collective-permute-start(bf16[8,128,128]{2,1,0:T(8,128)(2,1)S(1)} %slice.99), channel_id=1, source_target_pairs={{0,16},{16,32},{32,48},{48,64},{64,80},{80,96},{96,112},{112,0},{1... | collective-permute-start | bytes 786440 | tf_op jit(solution)/shard_map/ppermute | solution.py:17
  169.5 34.4 %all-to-all-start.1 = ((f32[128,4,128]{2,1,0:T(4,128)}), f32[128,4,128]{2,1,0:T(4,128)S(1)}, u32[]{:S(2)}, u32[]{:S(2)}) async-start(f32[128,4,128]{2,1,0:T(4,128)} %bitcast.23), calls=%async_computation.1 | async-start | bytes 524288 | tf_op jit(solution)/shard_map/all_to_all | solution.py:395
  (25 other events, 189.5 us)
